TPU v7x, 32 devices: a whole 2x2x4 slice. The times are simulated.
32 devices in a mesh: dom: 8 (over z, x), tp: 4 (over y, core).
Axes of the slice: x: 2, y: 2, z: 4, core: 2. Of those that a mesh axis runs over, the one named last changes fastest.
Arguments:
- state: bfloat16 [2, 8192, 512], P(None, 'dom'), may hold values from -6 to 6
- norm_gain: float32 [2, 2, 512], replicated, may hold values from 0.1 to 1.9
- norm_shift: float32 [2, 2, 512], replicated, may hold values from -3 to 3
- qkv_weight: bfloat16 [512, 3, 512], P(None, None, 'tp'), may hold values from -0.5 to 0.5
- out_weight: bfloat16 [512, 512], P('tp'), may hold values from -0.25 to 0.25
- up_weight: bfloat16 [512, 2048], P(None, 'tp'), may hold values from -0.25 to 0.25
- down_weight: bfloat16 [2048, 512], P('tp'), may hold values from -0.125 to 0.125
- neighbours: int32 [64, 8], P('dom'), may hold values from 0 to 63, as said below
- counts: int32 [64], P('dom'), may hold values from 2 to 8, as said below
Outputs:
- layer_out: bfloat16 [2, 8192, 512], P(None, 'dom', 'tp')
Inputs may be any that keep to these rules, and one draw needn't show every extreme that they name: `neighbours`: entry 0 of row b is b itself; the other 7 entries are distinct blocks whose partition (block // 8) lies at most two partitions before or after b's on a closed chain of partitions, block numbers taken modulo 64. `counts`: every partition has a block whose count is 8.
All inputs are finite; a program needn't handle non-finite values.
Results may differ from a plain program's by a relative error of at most 0.017.
Values may be sent and summed in bfloat16 or wider, within the bound.
A program may use at most 64 MiB of HBM per device.

v0:
```python
import math

import jax
import jax.numpy as jnp
from jax import lax
from jax.sharding import PartitionSpec as P

HEADS = 4
NODE_BLK = 128
KMAX = 8


def with_halo(value, sides, width):
    for axis, dim in sides:
        peers, length = (lax.axis_size(axis), value.shape[dim])
        up = [(i, (i + 1) % peers) for i in range(peers)]
        down = [(j, i) for i, j in up]
        last = lax.slice_in_dim(value, length - width, length, axis=dim)
        leading = lax.slice_in_dim(value, 0, width, axis=dim)
        before = lax.ppermute(last, axis, up)
        after = lax.ppermute(leading, axis, down)
        value = jnp.concatenate([before, value, after], axis=dim)
    return value


def shifted(block, axis, distance):
    devices = range(lax.axis_size(axis))
    route = [((i - distance) % len(devices), i) for i in devices]
    return lax.ppermute(block, axis, route)


def layer_norm(values, gain_row, shift_row):
    row_mean = jnp.mean(values, axis=-1, keepdims=True)
    centred = values - row_mean
    spread = jnp.mean(centred * centred, axis=-1, keepdims=True)
    return centred * lax.rsqrt(spread + 1e-05) * gain_row + shift_row


def local(
    state, norm_gain, norm_shift, qkv_weight, out_weight, up_weight, down_weight, neighbours, counts
):
    samples, row_count, feat_width = state.shape
    per_dev = row_count // NODE_BLK
    block_count = per_dev * lax.axis_size("dom")
    head_cols = qkv_weight.shape[2]
    head_size = feat_width // HEADS
    heads_here = head_cols // head_size
    tp_rank = lax.axis_index("tp")
    resid_in = state.astype(jnp.float32)
    normed = layer_norm(resid_in, norm_gain[0][:, None, :], norm_shift[0][:, None, :]).astype(
        jnp.bfloat16
    )
    normed = normed.reshape(samples, per_dev, NODE_BLK, feat_width)
    projected = jnp.einsum(
        "sbnd,dce->bsnce", normed, qkv_weight, preferred_element_type=jnp.float32
    ).astype(jnp.bfloat16)
    query_heads = projected[:, :, :, 0].reshape(per_dev, samples, NODE_BLK, heads_here, head_size)
    own_pairs = projected[:, :, :, 1:].reshape(per_dev, samples, NODE_BLK, 2 * head_cols)
    near_side = with_halo(own_pairs, (("dom", 0),), per_dev)
    far_side = [shifted(own_pairs, "dom", offset) for offset in (2, -2)]
    window = jnp.concatenate([far_side[0], near_side, far_side[1]], axis=0)
    first_block = lax.axis_index("dom") * per_dev - 2 * per_dev
    window_idx = jnp.mod(neighbours - first_block, block_count)
    chosen = window[window_idx]
    key_rows = chosen[..., :head_cols].reshape(
        per_dev, KMAX, samples, NODE_BLK, heads_here, head_size
    )
    value_rows = chosen[..., head_cols:].reshape(
        per_dev, KMAX, samples, NODE_BLK, heads_here, head_size
    )
    scores = jnp.einsum(
        "bsqhe,bjskhe->bshqjk", query_heads, key_rows, preferred_element_type=jnp.float32
    ) / math.sqrt(head_size)
    live_mask = jnp.arange(KMAX, dtype=jnp.int32)[None, :] < counts[:, None]
    masked = jnp.where(live_mask[:, None, None, None, :, None], scores, -1e30)
    row_top = jnp.max(masked, axis=(4, 5), keepdims=True)
    weights = jnp.exp(masked - row_top)
    weights = (weights / jnp.sum(weights, axis=(4, 5), keepdims=True)).astype(jnp.bfloat16)
    mixed_heads = jnp.einsum(
        "bshqjk,bjskhe->sbqhe", weights, value_rows, preferred_element_type=jnp.float32
    ).astype(jnp.bfloat16)
    mixed_heads = mixed_heads.reshape(samples, row_count, head_cols)
    partial_value = jnp.einsum(
        "sre,ed->srd", mixed_heads, out_weight, preferred_element_type=jnp.float32
    )
    attn_sum = lax.psum(partial_value.astype(jnp.bfloat16), "tp").astype(jnp.float32)
    residual = resid_in + attn_sum
    normed2 = layer_norm(residual, norm_gain[1][:, None, :], norm_shift[1][:, None, :]).astype(
        jnp.bfloat16
    )
    hidden = jax.nn.silu(
        jnp.einsum("srd,df->srf", normed2, up_weight, preferred_element_type=jnp.float32)
    ).astype(jnp.bfloat16)
    update = jnp.einsum("srf,fd->srd", hidden, down_weight, preferred_element_type=jnp.float32)
    update = lax.psum_scatter(
        update.astype(jnp.bfloat16), "tp", scatter_dimension=2, tiled=True
    ).astype(jnp.float32)
    col_share = update.shape[2]
    kept_cols = lax.dynamic_slice_in_dim(residual, tp_rank * col_share, col_share, 2)
    return (kept_cols + update).astype(jnp.bfloat16)


def solution(mesh):
    placed = (
        P(None, "dom", None),
        P(),
        P(),
        P(None, None, "tp"),
        P("tp", None),
        P(None, "tp"),
        P("tp", None),
        P("dom", None),
        P("dom"),
    )
    return jax.shard_map(
        local, mesh=mesh, in_specs=placed, out_specs=P(None, "dom", "tp"), check_vma=False
    )
```

profile of v0, /device:TPU:1, one launch (start us, length us, event | category | flops | bytes accessed | tf_op | source)
XLA Modules:
  0.0 232.3 jit_solution(1990845470973341466)
XLA Ops:
  6.5 0.0 copy-start
  6.5 0.0 all-reduce.2.cloned.1.call-start
  6.6 2.1 convert_reduce_fusion
  8.7 2.4 %fusion.4 = f32[2,1024]{1,0:T(2,128)S(1)} fusion(bf16[2,1024,512]{2,1,0:T(8,128)(2,1)} %param.9, f32[2,1024]{1,0:T(2,128)S(1)} %broadcast_multiply_fusion.1), kind=kLoop, calls=%fused_computation.11 | loop fusion | flops 4192256 | bytes 2113536 | tf_op jit(solution)/shard_map/reduce_sum | solution.py:35
  11.2 0.0 copy-done.1
  11.2 0.9 fusion.7
  12.2 0.0 copy-start.8
  12.2 0.0 copy-start.11
  12.2 1.0 fusion.20
  13.2 1.1 copy-done.4
  14.4 1.1 slice.34
  15.5 2.3 copy.30
  17.7 2.1 collective-permute-start
  19.9 1.2 collective-permute-start.1
  21.1 3.0 %collective-permute-start.2 = (bf16[8,2,128,256]{3,2,1,0:T(8,128)(2,1)}, bf16[8,2,128,256]{3,2,1,0:T(8,128)(2,1)}, u32[]{:S(2)}, u32[]{:S(2)}) collective-permute-start(bf16[8,2,128,256]{3,2,1,0:T(8,128)(2,1)} %copy.30), channel_id=1, source_target_pairs={{4,0},{8,4},{12,8},{16,12},{20,16},{24,20},{28,24},{0,28},{5,1},{9... | collective-permute-start | bytes 3145736 | tf_op jit(solution)/shard_map/ppermute | solution.py:21
  24.0 0.3 collective-permute-start.3
  24.3 0.1 reshape.95
  24.4 0.0 copy-done.11
  24.4 0.1 iota_compare_fusion
  24.5 20.6 %collective-permute-done = bf16[8,2,128,256]{3,2,1,0:T(8,128)(2,1)} collective-permute-done((bf16[8,2,128,256]{3,2,1,0:T(8,128)(2,1)}, bf16[8,2,128,256]{3,2,1,0:T(8,128)(2,1)}, u32[]{:S(2)}, u32[]{:S(2)}) %collective-permute-start) | collective-permute-done | bytes 1048608 | tf_op jit(solution)/shard_map/ppermute | solution.py:29
  45.1 2.4 %constant_dynamic-update-slice_fusion.4 = bf16[40,2,128,256]{3,2,1,0:T(8,128)(2,1)} fusion(bf16[8,2,128,256]{3,2,1,0:T(8,128)(2,1)} %collective-permute-done), kind=kLoop, calls=%fused_computation.47 | loop fusion | bytes 2097152
  47.5 20.8 %collective-permute-done.1 = bf16[8,2,128,256]{3,2,1,0:T(8,128)(2,1)} collective-permute-done((bf16[8,2,128,256]{3,2,1,0:T(8,128)(2,1)}, bf16[8,2,128,256]{3,2,1,0:T(8,128)(2,1)}, u32[]{:S(2)}, u32[]{:S(2)}) %collective-permute-start.1) | collective-permute-done | bytes 1048608 | tf_op jit(solution)/shard_map/ppermute | solution.py:20
  68.3 2.3 constant_dynamic-update-slice_fusion.3
  70.6 1.0 constant_dynamic-update-slice_fusion.2
  71.6 0.0 collective-permute-done.2
  71.6 2.3 constant_dynamic-update-slice_fusion.1
  73.9 16.9 %collective-permute-done.3 = bf16[8,2,128,256]{3,2,1,0:T(8,128)(2,1)} collective-permute-done((bf16[8,2,128,256]{3,2,1,0:T(8,128)(2,1)}, bf16[8,2,128,256]{3,2,1,0:T(8,128)(2,1)}, u32[]{:S(2)}, u32[]{:S(2)}) %collective-permute-start.3) | collective-permute-done | bytes 1048608 | tf_op jit(solution)/shard_map/ppermute | solution.py:29
  90.8 2.4 %constant_dynamic-update-slice_fusion = bf16[40,2,128,256]{3,2,1,0:T(8,128)(2,1)} fusion(bf16[40,2,128,256]{3,2,1,0:T(8,128)(2,1)} %constant_dynamic-update-slice_fusion.1, bf16[8,2,128,256]{3,2,1,0:T(8,128)(2,1)} %collective-permute-done.3), kind=kLoop, calls=%fused_computation.43 | loop fusion | bytes 2097152 | tf_op jit(solution)/shard_map/concatenate | solution.py:61
  93.1 8.0 %gather_fusion = bf16[64,2,128,256]{3,2,1,0:T(8,128)(2,1)} fusion(bf16[40,2,128,256]{3,2,1,0:T(8,128)(2,1)} %constant_dynamic-update-slice_fusion, s32[1024]{0:T(1024)S(1)} %pad_clamp_fusion), kind=kCustom, calls=%fused_computation | custom fusion | bytes 16777472 | tf_op jit(solution)/shard_map/gather | solution.py:64
  101.1 3.8 %fusion.40 = (bf16[8,8,2,128,128]{4,3,2,1,0:T(8,128)(2,1)S(1)}, bf16[8,8,2,128,128]{4,3,2,1,0:T(8,128)(2,1)S(1)}) fusion(bf16[8,8,2,128,256]{4,3,2,1,0:T(8,128)(2,1)} %bitcast.52), kind=kLoop, calls=%fused_computation.64 | loop fusion | bytes 16777216 | tf_op jit(solution)/shard_map/slice | solution.py:68
  104.9 2.4 %fusion = (f32[8,2,128]{2,1,0:T(2,128)S(1)}, f32[8,2,128,8,128]{2,4,3,1,0:T(8,128)S(1)}) fusion(pred[8,8]{1,0:T(8,128)(4,1)S(1)} %iota_compare_fusion, bf16[8,8,2,128,128]{4,3,2,1,0:T(8,128)(2,1)S(1)} %get-tuple-element.6, bf16[8,2,128,3,128]{2,4,3,0,1:T(8,128)(2,1)} %copy-done.4), kind=kOutput, calls=%fused_computation.4 | convolution fusion | flops 543160320 | bytes 13115456 | tf_op jit(solution)/shard_map/bsqhe,bjskhe->bshqjk/dot_general | solution.py:71
  107.3 2.0 fusion.1
  109.3 0.0 copy-start.5
  109.3 2.8 %fusion.26 = bf16[2,8,128,128]{2,3,1,0:T(8,128)(2,1)S(1)} fusion(bf16[8,8,2,128,128]{4,3,2,1,0:T(8,128)(2,1)S(1)} %get-tuple-element.5, f32[8,2,128,8,128]{2,4,3,1,0:T(8,128)S(1)} %get-tuple-element.14, f32[8,2,128]{2,1,0:T(2,128)S(1)} %fusion.1, f32[8,2,128]{2,1,0:T(2,128)S(1)} %get-tuple-element.13, pred[8,8]{1,0:T(8,128)(4,1)S(1)} %iota_compare_fusion), kind=kOutput, calls=%fused_computation.34 | convolution fusion | flops 547618816 | bytes 13123648 | tf_op jit(solution)/shard_map/bshqjk,bjskhe->sbqhe/dot_general | solution.py:79
  112.1 2.0 convolution_convert_fusion
  114.2 0.0 all-reduce.2.cloned.1.call-update
  114.2 0.2 reduce-scatter.4.cloned.1.call-start
  114.4 57.5 %all-reduce.2.cloned.1.call-done = bf16[2,1024,512]{2,1,0:T(8,128)(2,1)} async-done(((bf16[2,1024,512]{2,1,0:T(8,128)(2,1)}), bf16[2,1024,512]{2,1,0:T(8,128)(2,1)}) %all-reduce.2.cloned.1.call-update) | async-done | bytes 2097168 | tf_op jit(solution)/shard_map/psum | solution.py:86
  171.9 4.2 %convert_add_fusion = (f32[2,1024,512]{2,1,0:T(8,128)}, f32[2,1024]{1,0:T(2,128)S(1)}) fusion(bf16[2,1024,512]{2,1,0:T(8,128)(2,1)S(1)} %copy-done.1, bf16[2,1024,512]{2,1,0:T(8,128)(2,1)} %all-reduce.2.cloned.1.call-done), kind=kLoop, calls=%fused_computation.6 | loop fusion | flops 4192256 | bytes 8396800 | tf_op jit(solution)/shard_map/add | solution.py:87
  176.2 1.0 multiply_reduce_fusion
  177.2 5.5 %fusion.19 = bf16[2,1024,512]{2,1,0:T(8,128)(2,1)} fusion(f32[2,512]{1,0:T(2,128)S(1)} %get-tuple-element.12, f32[2,512]{1,0:T(2,128)S(1)} %get-tuple-element.15, f32[2,1024]{1,0:T(2,128)S(1)} %add_rsqrt_fusion, f32[2,1024]{1,0:T(2,128)S(1)} %broadcast_multiply_fusion, bf16[512,512]{1,0:T(8,128)(2,1)S(1)} %copy-done, bf16[512,512]{1,0:T(8,128)(2,1)S(1)} %copy-done.9, ...), kind=kOutput, calls=%fused_computation.29 | convolution fusion | flops 2162163712 | bytes 7364608 | tf_op jit(solution)/shard_map/srf,fd->srd/dot_general | solution.py:94
  182.7 5.0 %copy.48 = bf16[2,1024,512]{1,0,2:T(2,128)(2,1)S(1)} copy(bf16[2,1024,512]{2,1,0:T(8,128)(2,1)} %fusion.19) | data formatting | bytes 4194304
  187.7 1.9 copy.52
  189.7 0.0 reduce-scatter.4.cloned.1.call-update
  189.7 31.7 %reduce-scatter.4.cloned.1.call-done = bf16[128,2048]{1,0:T(8,128)(2,1)} async-done(((bf16[512,2048]{1,0:T(8,128)(2,1)}), bf16[128,2048]{1,0:T(8,128)(2,1)}) %reduce-scatter.4.cloned.1.call-update) | async-done | bytes 524304
  221.4 1.4 reshape.111
  222.8 0.5 copy.49
  223.3 2.1 add_convert_fusion.6
  (24 shorter events, 0.1 us)
Async XLA Ops:
  6.5 170.7 %copy-start = (bf16[512,512]{1,0:T(8,128)(2,1)S(1)}, bf16[512,512]{1,0:T(8,128)(2,1)}, u32[]{:S(2)}) copy-start(bf16[512,512]{1,0:T(8,128)(2,1)} %param.15) | copy-start | bytes 1572868
  6.5 4.7 %copy-start.1 = (bf16[2,1024,512]{2,1,0:T(8,128)(2,1)S(1)}, bf16[2,1024,512]{2,1,0:T(8,128)(2,1)}, u32[]{:S(2)}) copy-start(bf16[2,1024,512]{2,1,0:T(8,128)(2,1)} %param.9) | copy-start | bytes 6291460
  6.5 4.6 %copy-start.6 = (f32[2,2,512]{2,1,0:T(2,128)S(1)}, f32[2,2,512]{2,1,0:T(2,128)}, u32[]{:S(2)}) copy-start(f32[2,2,512]{2,1,0:T(2,128)} %param.11) | copy-start | bytes 24580
  6.5 4.6 %copy-start.7 = (f32[2,2,512]{2,1,0:T(2,128)S(1)}, f32[2,2,512]{2,1,0:T(2,128)}, u32[]{:S(2)}) copy-start(f32[2,2,512]{2,1,0:T(2,128)} %param.10) | copy-start | bytes 24580
  6.5 5.6 %copy-start.10 = (bf16[512,3,128]{2,0,1:T(8,128)(2,1)S(1)}, bf16[512,3,128]{2,0,1:T(8,128)(2,1)}, u32[]{:S(2)}) copy-start(bf16[512,3,128]{2,0,1:T(8,128)(2,1)} %param.12) | copy-start | bytes 1179652
  6.5 165.4 %all-reduce.2.cloned.1.call-start = ((), (), s32[]{:S(2)}) async-start(), calls=%async_computation.1 | async-start | bytes 4194304 | tf_op jit(solution)/shard_map/psum | solution.py:86
  12.2 12.1 %copy-start.8 = (s32[8,8]{1,0:T(8,128)S(1)}, s32[8,8]{1,0:T(8,128)}, u32[]{:S(2)}) copy-start(s32[8,8]{1,0:T(8,128)} %param.16) | copy-start | bytes 772
  12.2 12.2 %copy-start.11 = (s32[8]{0:T(128)S(1)}, s32[8]{0:T(128)}, u32[]{:S(2)}) copy-start(s32[8]{0:T(128)} %param.17) | copy-start | bytes 100
  13.2 1.2 copy-start.4
  17.7 27.4 %collective-permute-start = (bf16[8,2,128,256]{3,2,1,0:T(8,128)(2,1)}, bf16[8,2,128,256]{3,2,1,0:T(8,128)(2,1)}, u32[]{:S(2)}, u32[]{:S(2)}) collective-permute-start(bf16[8,2,128,256]{3,2,1,0:T(8,128)(2,1)} %copy.30), channel_id=1, source_target_pairs={{24,0},{28,4},{0,8},{4,12},{8,16},{12,20},{16,24},{20,28},{25,1},{... | collective-permute-start | bytes 3145736 | tf_op jit(solution)/shard_map/ppermute | solution.py:29
  19.9 48.4 %collective-permute-start.1 = (bf16[8,2,128,256]{3,2,1,0:T(8,128)(2,1)}, bf16[8,2,128,256]{3,2,1,0:T(8,128)(2,1)}, u32[]{:S(2)}, u32[]{:S(2)}) collective-permute-start(bf16[8,2,128,256]{3,2,1,0:T(8,128)(2,1)} %copy.30), channel_id=1, source_target_pairs={{0,4},{4,8},{8,12},{12,16},{16,20},{20,24},{24,28},{28,0},{1,5},{5... | collective-permute-start | bytes 3145736 | tf_op jit(solution)/shard_map/ppermute | solution.py:20
  21.1 50.5 %collective-permute-start.2 = (bf16[8,2,128,256]{3,2,1,0:T(8,128)(2,1)}, bf16[8,2,128,256]{3,2,1,0:T(8,128)(2,1)}, u32[]{:S(2)}, u32[]{:S(2)}) collective-permute-start(bf16[8,2,128,256]{3,2,1,0:T(8,128)(2,1)} %copy.30), channel_id=1, source_target_pairs={{4,0},{8,4},{12,8},{16,12},{20,16},{24,20},{28,24},{0,28},{5,1},{9... | collective-permute-start | bytes 3145736 | tf_op jit(solution)/shard_map/ppermute | solution.py:21
  24.0 66.7 %collective-permute-start.3 = (bf16[8,2,128,256]{3,2,1,0:T(8,128)(2,1)}, bf16[8,2,128,256]{3,2,1,0:T(8,128)(2,1)}, u32[]{:S(2)}, u32[]{:S(2)}) collective-permute-start(bf16[8,2,128,256]{3,2,1,0:T(8,128)(2,1)} %copy.30), channel_id=1, source_target_pairs={{8,0},{12,4},{16,8},{20,12},{24,16},{28,20},{0,24},{4,28},{9,1},{1... | collective-permute-start | bytes 3145736 | tf_op jit(solution)/shard_map/ppermute | solution.py:29
  24.4 46.2 %copy-start.3 = (bf16[8,2,128,256]{3,2,1,0:T(8,128)(2,1)S(1)}, bf16[8,2,128,256]{3,2,1,0:T(8,128)(2,1)}, u32[]{:S(2)}) copy-start(bf16[8,2,128,256]{3,2,1,0:T(8,128)(2,1)} %copy.30) | copy-start | bytes 3145732
  109.3 2.8 %copy-start.5 = (bf16[128,512]{1,0:T(8,128)(2,1)S(1)}, bf16[128,512]{1,0:T(8,128)(2,1)}, u32[]{:S(2)}) copy-start(bf16[128,512]{1,0:T(8,128)(2,1)} %param.13) | copy-start | bytes 393220
  114.2 107.2 %reduce-scatter.4.cloned.1.call-start = ((), (), s32[]{:S(2)}) async-start(), calls=%async_computation.2 | async-start | bytes 2621440
  171.9 4.2 %copy-start.2 = (bf16[2,1024,512]{2,1,0:T(8,128)(2,1)S(1)}, bf16[2,1024,512]{2,1,0:T(8,128)(2,1)}, u32[]{:S(2)}) copy-start(bf16[2,1024,512]{2,1,0:T(8,128)(2,1)} %all-reduce.2.cloned.1.call-done) | copy-start | bytes 6291460
  176.2 1.0 copy-start.9
Sparse Core Ops, SparseCore 0:
  114.3 57.5 all-reduce.1
  189.8 31.5 reduce-scatter.3
where the time goes:
time: 234 us; the launch traced here: 232 us
  waiting for transfers between devices  148 us (63%)
  local copies, waits for them, and re-layouts  35.7 us (15%)
  other arithmetic  14.9 us (6%)
  matrix products  13.7 us (6%)
  between operations  13.6 us (6%)
  starting transfers between devices  6.81 us (3%)
    psum x1, waiting for transfers between devices, local(): lax.psum(partial_value.astype(jnp.bfloat16), 'tp').astype(jnp.float32)  57.5 us
    ppermute x2, waiting for transfers between devices, shifted(): return lax.ppermute(block, axis, route)  37.5 us
    unnamed x3, waiting for transfers between devices  31.7 us
    ppermute x1, waiting for transfers between devices, with_halo(): before = lax.ppermute(last, axis, up)  20.8 us
    unnamed x32, local copies, waits for them, and re-layouts  18.1 us
    gather x1, local copies, waits for them, and re-layouts, local(): chosen = window[window_idx]  8.01 us
    dot_general x1, matrix products, local(): jnp.einsum('srf,fd->srd', hidden, down_weight, preferred_element_type=jnp...  5.48 us
  transfers between devices with their start and end apart: 6, of which 5 were waited for; matrix products, arithmetic and copies ran while one was open for 4% of the time, Pallas kernels for 0%

commit v1 on v0

v1 whole, which is shorter than its diff:
```python
import math

import jax
import jax.numpy as jnp
from jax import lax
from jax.experimental import pallas as pl
from jax.experimental.pallas import tpu as pltpu
from jax.sharding import PartitionSpec as P

HEADS = 4
NODE_BLK = 128
KMAX = 8
FAR = 3


def layer_norm(values, gain_row, shift_row):
    row_mean = jnp.mean(values, axis=-1, keepdims=True)
    centred = values - row_mean
    spread = jnp.mean(centred * centred, axis=-1, keepdims=True)
    return centred * lax.rsqrt(spread + 1e-05) * gain_row + shift_row


def layer_kernel(
    slots, live, state, gain, shift, wqkv, wout, wup, wdown, out,
    nrm, kv, query, heads, outgoing, wout_all, wup_all, wdown_all, resid, normed2, total, cols,
    z_s, z_r, y_s, y_r, a_s, a_r, b_s, b_r, n_s, n_r, m_s, m_r, wy_s, wy_r, wa_s, wa_r, wb_s, wb_r,
    h_s, h_r, o_s, o_r,
):
    d = lax.axis_index("dom")
    t = lax.axis_index("tp")
    doms = lax.axis_size("dom")
    odd = lax.rem(d, 2)
    near = d + 1 - 2 * odd
    diag = lax.rem(d - 1 + 2 * odd + doms, doms)
    plus = lax.rem(d + 2, doms)
    minus = lax.rem(d + doms - 2, doms)
    core = lax.rem(t, 2)
    sib = t + 1 - 2 * core
    across = lax.rem(t + 2, 4)
    corner = lax.rem(sib + 2, 4)
    targets = (diag, minus, plus)
    f32 = jnp.float32

    def remote(src, dst, send, recv, dd, tt):
        return pltpu.make_async_remote_copy(
            src_ref=src, dst_ref=dst, send_sem=send, recv_sem=recv, device_id=(dd, tt),
            device_id_type=pl.DeviceIdType.MESH,
        )

    barrier = pltpu.get_barrier_semaphore()
    partners = [(near, t), (diag, t), (plus, t), (minus, t), (d, sib), (d, across), (d, corner)]
    for partner in partners:
        pl.semaphore_signal(
            barrier, inc=1, device_id=partner, device_id_type=pl.DeviceIdType.MESH
        )

    def norm_one(u, carry):
        s = u // 8
        nrm[u] = layer_norm(state[u].astype(f32), gain[0, s], shift[0, s]).astype(jnp.bfloat16)
        return carry

    lax.fori_loop(0, 16, norm_one, 0)
    pl.semaphore_wait(barrier, 7)

    def z_copy(f, i):
        return remote(
            nrm.at[4 * t + i], nrm.at[(2 + f) * 16 + 4 * t + i], z_s.at[f, i], z_r.at[f, i],
            targets[f], t,
        )

    def y_copy(f, i, owner=t):
        u = (2 + f) * 16 + 4 * owner + i
        return remote(nrm.at[u], nrm.at[u], y_s.at[f, i], y_r.at[f, i], d, across)

    def a_copy(f, i, owner=t):
        u = (2 + f) * 16 + 4 * owner + i
        return remote(nrm.at[u], nrm.at[u], a_s.at[f, i], a_r.at[f, i], d, sib)

    def b_copy(f, i, owner=across):
        u = (2 + f) * 16 + 4 * owner + i
        return remote(nrm.at[u], nrm.at[u], b_s.at[f, i], b_r.at[f, i], d, sib)

    def n_copy(i):
        u = 8 * core + 2 * i
        return remote(
            nrm.at[pl.ds(u, 2)], nrm.at[pl.ds(16 + u, 2)], n_s.at[i], n_r.at[i], near, t
        )

    def m_copy(i, side=core):
        u = 16 + 8 * side + 2 * i
        return remote(nrm.at[pl.ds(u, 2)], nrm.at[pl.ds(u, 2)], m_s.at[i], m_r.at[i], d, sib)

    shards = ((wout, wout_all), (wup, wup_all), (wdown, wdown_all))

    def wy_copy(k, owner=t):
        return remote(shards[k][0], shards[k][1].at[owner], wy_s.at[k], wy_r.at[k], d, across)

    def wa_copy(k, owner=t):
        return remote(shards[k][0], shards[k][1].at[owner], wa_s.at[k], wa_r.at[k], d, sib)

    def wb_copy(k, owner=across):
        full = shards[k][1]
        return remote(full.at[owner], full.at[owner], wb_s.at[k], wb_r.at[k], d, sib)

    def send_all(i, carry):
        for f in range(FAR):
            z_copy(f, i).start()
        n_copy(i).start()
        return carry

    lax.fori_loop(0, 4, send_all, 0)
    for k in range(3):
        wa_copy(k).start()
    for shard, full in shards:
        full[t] = shard[...]

    def project_own(u, carry):
        made = jnp.dot(nrm[u], wqkv[...], preferred_element_type=f32).astype(jnp.bfloat16)
        query[u] = made[:, :128]
        kv[u] = made[:, 128:]
        return carry

    lax.fori_loop(0, 16, project_own, 0)

    def project(u):
        kv[u] = jnp.dot(nrm[u], wqkv[:, 128:], preferred_element_type=f32).astype(jnp.bfloat16)

    def relay(i, carry):
        @pl.when(i < 4)
        def _():
            for f in range(FAR):
                z_copy(f, i).wait_recv()
                y_copy(f, i).start()
                a_copy(f, i).start()
            n_copy(i).wait_recv()
            m_copy(i).start()
            for f in range(FAR):
                project((2 + f) * 16 + 4 * t + i)

        @pl.when(i > 0)
        def _():
            for f in range(FAR):
                y_copy(f, i - 1, across).wait_recv()
                b_copy(f, i - 1).start()
            for f in range(FAR):
                project((2 + f) * 16 + 4 * across + i - 1)

        return carry

    lax.fori_loop(0, 5, relay, 0)
    for k in range(3):
        wy_copy(k).start()

    def take_sib(i, carry):
        for f in range(FAR):
            a_copy(f, i, sib).wait_recv()
        m_copy(i, 1 - core).wait_recv()
        for f in range(FAR):
            project((2 + f) * 16 + 4 * sib + i)
        for r in range(2):
            project(16 + 8 * core + 2 * i + r)
            project(16 + 8 * (1 - core) + 2 * i + r)
        return carry

    lax.fori_loop(0, 4, take_sib, 0)

    def take_corner(i, carry):
        for f in range(FAR):
            b_copy(f, i, corner).wait_recv()
        for f in range(FAR):
            project((2 + f) * 16 + 4 * corner + i)
        return carry

    lax.fori_loop(0, 4, take_corner, 0)

    scale = 1.0 / math.sqrt(128)
    lane_entry = lax.broadcasted_iota(jnp.int32, (1, KMAX * NODE_BLK), 1) // NODE_BLK

    def attend(b, s):
        q = query[s * 8 + b]
        places = [slots[b, j] + s * 8 for j in range(KMAX)]
        scores = jnp.concatenate(
            [
                lax.dot_general(
                    q, kv[places[j], :, :128], (((1,), (1,)), ((), ())),
                    preferred_element_type=f32,
                )
                for j in range(KMAX)
            ],
            axis=1,
        )
        scores = jnp.where(lane_entry < live[b], scores, -1e30)
        top = jnp.max(scores, axis=1, keepdims=True)
        weights = jnp.exp((scores - top) * scale)
        whole = jnp.sum(weights, axis=1, keepdims=True)
        weights = weights.astype(jnp.bfloat16)
        mixed = jnp.zeros((NODE_BLK, 128), f32)
        for j in range(KMAX):
            mixed += jnp.dot(
                weights[:, j * 128 : (j + 1) * 128], kv[places[j], :, 128:],
                preferred_element_type=f32,
            )
        return (mixed / whole).astype(jnp.bfloat16)

    def h_copy(k, src_tp=t):
        owner = lax.rem(t + 1 + k // 2, 4)
        place = lax.rem(k, 2) * 256
        return remote(
            outgoing.at[k], heads.at[src_tp, pl.ds(place, 256)], h_s.at[k], h_r.at[k], d, owner
        )

    def attend_away(k, carry):
        b = lax.rem(2 * (t + 1) + k, 8)
        for s in range(2):
            outgoing[k, s * 128 : (s + 1) * 128] = attend(b, s)
        h_copy(k).start()
        return carry

    lax.fori_loop(0, 6, attend_away, 0)

    def attend_here(r, carry):
        for s in range(2):
            heads[t, pl.ds(pl.multiple_of(r * 256 + s * 128, 128), 128)] = attend(2 * t + r, s)
        return carry

    lax.fori_loop(0, 2, attend_here, 0)

    for k in range(3):
        wy_copy(k, across).wait_recv()
        wb_copy(k).start()
    for k in range(6):
        h_copy(k, lax.rem(t + 3 - k // 2, 4)).wait_recv()
    wa_copy(0, sib).wait_recv()
    wb_copy(0, corner).wait_recv()

    for lu in range(4):
        r, s = lu // 2, lu % 2
        rows = slice(lu * 128, (lu + 1) * 128)
        attn = jnp.zeros((128, 512), f32)
        for h in range(HEADS):
            attn += (
                jnp.dot(heads[h, rows], wout_all[h], preferred_element_type=f32)
                .astype(jnp.bfloat16)
                .astype(f32)
            )
        after = state[s * 8 + 2 * t + r].astype(f32) + attn
        resid[rows] = after
        normed2[rows] = layer_norm(after, gain[1, s], shift[1, s]).astype(jnp.bfloat16)
    total[...] = jnp.zeros_like(total)

    def mlp(g):
        for half in range(2):
            rows = slice(half * 256, (half + 1) * 256)
            pre = jnp.dot(normed2[rows], wup_all[g], preferred_element_type=f32)
            hidden = (pre / (1.0 + jnp.exp(-pre))).astype(jnp.bfloat16)
            term = jnp.dot(hidden, wdown_all[g], preferred_element_type=f32)
            total[rows] += term.astype(jnp.bfloat16).astype(f32)

    wa_copy(1, sib).wait_recv()
    wa_copy(2, sib).wait_recv()
    lax.fori_loop(0, 2, lambda k, c: (mlp(t - core + k), c)[1], 0)
    wb_copy(1, corner).wait_recv()
    wb_copy(2, corner).wait_recv()
    lax.fori_loop(0, 2, lambda k, c: (mlp(across - core + k), c)[1], 0)

    for j in range(4):
        lanes = slice(j * 128, (j + 1) * 128)
        cols[j] = (resid[:, lanes] + total[:, lanes]).astype(jnp.bfloat16)

    def o_copy(k, owner=t):
        peer = lax.rem(t + 1 + k, 4)
        return remote(cols.at[peer], out.at[owner], o_s.at[k], o_r.at[k], d, peer)

    for k in range(3):
        o_copy(k).start()
    out[t] = cols[t]
    for k in range(3):
        o_copy(k, lax.rem(t + 3 - k, 4)).wait_recv()

    def drain(i, carry):
        for f in range(FAR):
            z_copy(f, i).wait_send()
            y_copy(f, i).wait_send()
            a_copy(f, i).wait_send()
            b_copy(f, i).wait_send()
        n_copy(i).wait_send()
        m_copy(i).wait_send()
        return carry

    lax.fori_loop(0, 4, drain, 0)
    for k in range(3):
        wy_copy(k).wait_send()
        wa_copy(k).wait_send()
        wb_copy(k).wait_send()
        o_copy(k).wait_send()
    for k in range(6):
        h_copy(k).wait_send()


def local(
    state, norm_gain, norm_shift, qkv_weight, out_weight, up_weight, down_weight, neighbours, counts
):
    samples, row_count, feat = state.shape
    per_dev = row_count // NODE_BLK
    doms = lax.axis_size("dom")
    d = lax.axis_index("dom")
    odd = d % 2
    away = jnp.mod(neighbours // per_dev - d, doms)
    slot = jnp.where(away == 0, 0, 0)
    slot = jnp.where(away == 1, 1 + odd, slot)
    slot = jnp.where(away == doms - 1, 2 - odd, slot)
    slot = jnp.where(away == 2, 3, slot)
    slot = jnp.where(away == doms - 2, 4, slot)
    slots = (slot * 16 + neighbours % per_dev).astype(jnp.int32)
    bf16 = jnp.bfloat16
    dma = pltpu.SemaphoreType.DMA
    smem = pl.BlockSpec(memory_space=pltpu.SMEM)
    vmem = pl.BlockSpec(memory_space=pltpu.VMEM)
    pairs = []
    for shape in [(3, 4)] * 4 + [(4,)] * 2 + [(3,)] * 3 + [(6,), (3,)]:
        pairs += [dma(shape), dma(shape)]
    out = pl.pallas_call(
        layer_kernel,
        out_shape=jax.ShapeDtypeStruct((4, 512, 128), bf16),
        in_specs=[smem, smem] + [vmem] * 7,
        out_specs=vmem,
        scratch_shapes=[
            pltpu.VMEM((80, 128, 512), bf16),
            pltpu.VMEM((80, 128, 256), bf16),
            pltpu.VMEM((16, 128, 128), bf16),
            pltpu.VMEM((4, 512, 128), bf16),
            pltpu.VMEM((6, 256, 128), bf16),
            pltpu.VMEM((4, 128, 512), bf16),
            pltpu.VMEM((4, 512, 512), bf16),
            pltpu.VMEM((4, 512, 512), bf16),
            pltpu.VMEM((512, 512), jnp.float32),
            pltpu.VMEM((512, 512), bf16),
            pltpu.VMEM((512, 512), jnp.float32),
            pltpu.VMEM((4, 512, 128), bf16),
        ]
        + pairs,
        compiler_params=pltpu.CompilerParams(
            collective_id=0, has_side_effects=True, vmem_limit_bytes=50 * 2**20
        ),
    )(
        slots,
        counts,
        state.reshape(samples * per_dev, NODE_BLK, feat),
        norm_gain.reshape(2, 2, 1, feat),
        norm_shift.reshape(2, 2, 1, feat),
        qkv_weight.reshape(feat, -1),
        out_weight,
        up_weight,
        down_weight,
    )
    out = out.reshape(per_dev, samples, NODE_BLK, 128)
    return jnp.transpose(out, (1, 0, 2, 3)).reshape(samples, row_count, 128)


def solution(mesh):
    placed = (
        P(None, "dom", None),
        P(),
        P(),
        P(None, None, "tp"),
        P("tp", None),
        P(None, "tp"),
        P("tp", None),
        P("dom", None),
        P("dom"),
    )
    return jax.shard_map(
        local, mesh=mesh, in_specs=placed, out_specs=P(None, "dom", "tp"), check_vma=False
    )
```

time: 234 us -> 104 us (0.44)
  waiting for transfers between devices: 148 us -> 0 us
  Pallas kernels: 0 us -> 95.3 us
  local copies, waits for them, and re-layouts: 35.7 us -> 7.25 us
  other arithmetic: 14.9 us -> 0.71 us
  matrix products: 13.7 us -> 0 us
  between operations: 13.6 us -> 0.04 us
  starting transfers between devices: 6.81 us -> 0 us
    pallas_call x0 -> x1, Pallas kernels: none -> 95.3 us  [local(): pl.pallas_call(layer_kernel, out_shape=jax.ShapeDtypeStruct((4, 512, 128)...]
    ppermute x4 -> x0, waiting for transfers between devices: 58.3 us -> none  [the longest x2 37.5 us: shifted(): return lax.ppermute(block, axis, route)]
    psum x1 -> x0, waiting for transfers between devices: 57.5 us -> none  [local(): lax.psum(partial_value.astype(jnp.bfloat16), 'tp').astype(jnp.float32)]
    unnamed x3 -> x0, waiting for transfers between devices: 31.7 us -> none
    dot_general x5 -> x0, matrix products: 13.7 us -> none  [the longest x1 5.48 us: local(): jnp.einsum('srf,fd->srd', hidden, down_weight, preferred_element_type=jnp...]
    unnamed x32 -> x9, local copies, waits for them, and re-layouts: 18.1 us -> 4.8 us
    gather x1 -> x0, local copies, waits for them, and re-layouts: 8.01 us -> none  [local(): chosen = window[window_idx]]
    reduce_sum x4 -> x0, other arithmetic: 7.51 us -> none  [the longest x2 3.44 us: layer_norm(): spread = jnp.mean(centred * centred, axis=-1, keepdims=True)]
  transfers between devices with their start and end apart: 6 -> 0, of which waited for: 5 -> 0; matrix products, arithmetic and copies ran while one was open for 4% -> 0% of each run, Pallas kernels for 0% -> 0%
where the time goes in v1:
time: 104 us; the launch traced here: 103 us
  Pallas kernels  95.3 us (92%)
  local copies, waits for them, and re-layouts  7.25 us (7%)
    pallas_call x1, Pallas kernels, local(): pl.pallas_call(layer_kernel, out_shape=jax.ShapeDtypeStruct((4, 512, 128)...  95.3 us
    unnamed x9, local copies, waits for them, and re-layouts  4.8 us

profile of v1, /device:TPU:1, one launch (start us, length us, event | category | flops | bytes accessed | tf_op | source)
XLA Modules:
  0.0 103.3 jit_solution(15725602419319629608)
XLA Ops:
  0.0 0.7 fusion.2.slots
  0.7 0.7 reshape.19.gain
  1.4 0.7 reshape.20.shift
  2.1 1.2 %copy.12 = bf16[512,3,128]{0,2,1:T(8,128)(2,1)S(1)} copy(bf16[512,3,128]{2,0,1:T(8,128)(2,1)} %param.12) | data formatting | bytes 786432 | tf_op args[3]
  3.3 0.2 copy.13.wqkv
  3.5 0.0 copy-start
  3.5 1.0 copy-done
  4.6 0.0 copy-start.1
  4.6 1.0 %copy-done.1 = bf16[512,512]{1,0:T(8,128)(2,1)S(1)} copy-done((bf16[512,512]{1,0:T(8,128)(2,1)S(1)}, bf16[512,512]{1,0:T(8,128)(2,1)}, u32[]{:S(2)}) %copy-start.1) | copy-done | bytes 524312
  5.6 0.0 copy-start.2
  5.6 0.9 copy-done.2
  6.5 0.0 copy-start.3
  6.5 0.7 copy-done.3
  7.2 95.3 %shard_map.91 = bf16[4,512,128]{2,1,0:T(8,128)(2,1)S(1)} custom-call(s32[8,8]{1,0:T(8,128)S(1)} %fusion.2.slots, s32[8]{0:T(128)S(1)} %copy-done.3, bf16[16,128,512]{2,1,0:T(8,128)(2,1)} %bitcast.7, f32[2,2,1,512]{3,2,1,0:T(1,128)S(1)} %reshape.19.gain, f32[2,2,1,512]{3,2,1,0:T(1,128)S(1)} %reshape.20.shift, bf16[512,384]{1,0:T(8,128)(2,1)S(1)} %copy.13.wqkv, ...), custom_call_target="tpu_custom_call" | custom-call | tf_op jit(solution)/shard_map/pallas_call | solution.py:322
  102.5 0.8 copy.14
Async XLA Ops:
  3.5 1.0 %copy-start = (bf16[512,512]{1,0:T(8,128)(2,1)S(1)}, bf16[512,512]{1,0:T(8,128)(2,1)}, u32[]{:S(2)}) copy-start(bf16[512,512]{1,0:T(8,128)(2,1)} %wup.1) | copy-start | bytes 1572868
  4.6 1.0 %copy-start.1 = (bf16[512,512]{1,0:T(8,128)(2,1)S(1)}, bf16[512,512]{1,0:T(8,128)(2,1)}, u32[]{:S(2)}) copy-start(bf16[512,512]{1,0:T(8,128)(2,1)} %wdown.1) | copy-start | bytes 1572868
  5.6 0.9 copy-start.2
  6.5 0.7 copy-start.3

commit v2 on v1

v2 whole, which is shorter than its diff:
```python
import math

import jax
import jax.numpy as jnp
from jax import lax
from jax.experimental import pallas as pl
from jax.experimental.pallas import tpu as pltpu
from jax.sharding import PartitionSpec as P

HEADS = 4
NODE_BLK = 128
KMAX = 8
FLOWS = 3


def layer_norm(values, gain_row, shift_row):
    row_mean = jnp.mean(values, axis=-1, keepdims=True)
    centred = values - row_mean
    spread = jnp.mean(centred * centred, axis=-1, keepdims=True)
    return centred * lax.rsqrt(spread + 1e-05) * gain_row + shift_row


def layer_kernel(
    neigh, live, gain, shift, state_in, wqkv_in, wout_in, wup_in, wdown_in, out,
    state, wqkv_raw, wqkv, nrm, kv, query, heads, outgoing, wout_all, wup_all, wdown_all, normed2,
    cols, c_state, c_w,
    z_s, z_r, y_s, y_r, a_s, a_r, b_s, b_r, x_s, x_r, n_s, n_r, m_s, m_r,
    wy_s, wy_r, wa_s, wa_r, wx_s, wx_r, w0_s, w0_r, w1_s, w1_r, h_s, h_r, o_s, o_r,
):
    d = lax.axis_index("dom")
    t = lax.axis_index("tp")
    doms = lax.axis_size("dom")
    odd = lax.rem(d, 2)
    near = d + 1 - 2 * odd
    plus = lax.rem(d + 2, doms)
    minus = lax.rem(d + doms - 2, doms)
    core = lax.rem(t, 2)
    sib = t + 1 - 2 * core
    across = lax.rem(t + 2, 4)
    corner = lax.rem(sib + 2, 4)
    f32 = jnp.float32
    bf16 = jnp.bfloat16

    def remote(src, dst, send, recv, dd, tt):
        return pltpu.make_async_remote_copy(
            src_ref=src, dst_ref=dst, send_sem=send, recv_sem=recv, device_id=(dd, tt),
            device_id_type=pl.DeviceIdType.MESH,
        )

    barrier = pltpu.get_barrier_semaphore()
    for partner in [(near, t), (plus, t), (minus, t), (d, sib), (d, across), (d, corner)]:
        pl.semaphore_signal(
            barrier, inc=1, device_id=partner, device_id_type=pl.DeviceIdType.MESH
        )

    def state_copy(k):
        rows = pl.ds(4 * lax.rem(t + k, 4), 4)
        return pltpu.make_async_copy(state_in.at[rows], state.at[rows], c_state.at[k])

    shards = ((wout_in, wout_all), (wup_in, wup_all), (wdown_in, wdown_all))
    own_copies = [pltpu.make_async_copy(wqkv_in, wqkv_raw, c_w.at[3])] + [
        pltpu.make_async_copy(shard, full.at[t], c_w.at[k])
        for k, (shard, full) in enumerate(shards)
    ]
    for k in range(4):
        state_copy(k).start()
    for copy in own_copies:
        copy.start()

    def norm_quarter(k, carry):
        state_copy(k).wait()

        def norm_one(i, inner):
            u = 4 * lax.rem(t + k, 4) + i
            s = u // 8
            nrm[u] = layer_norm(
                state[u].astype(f32), gain[0, pl.ds(s, 1)], shift[0, pl.ds(s, 1)]
            ).astype(bf16)
            return inner

        lax.fori_loop(0, 4, norm_one, 0)
        return carry

    def z_copy(f, i):
        return remote(
            nrm.at[4 * t + i], nrm.at[(2 + f) * 16 + 4 * t + i], z_s.at[f - 1, i],
            z_r.at[f - 1, i], (minus, plus)[f - 1], t,
        )

    def x_copy(i):
        u = 4 * t + i
        return remote(
            nrm.at[(3 + odd) * 16 + u], nrm.at[2 * 16 + u], x_s.at[i], x_r.at[i], near, t
        )

    def y_copy(f, i, owner=t):
        u = (2 + f) * 16 + 4 * owner + i
        return remote(nrm.at[u], nrm.at[u], y_s.at[f, i], y_r.at[f, i], d, across)

    def a_copy(f, i, owner=t):
        u = (2 + f) * 16 + 4 * owner + i
        return remote(nrm.at[u], nrm.at[u], a_s.at[f, i], a_r.at[f, i], d, sib)

    def b_copy(f, i, owner=across):
        u = (2 + f) * 16 + 4 * owner + i
        return remote(nrm.at[u], nrm.at[u], b_s.at[f, i], b_r.at[f, i], d, sib)

    def n_copy(i):
        u = 8 * core + 2 * i
        return remote(
            nrm.at[pl.ds(u, 2)], nrm.at[pl.ds(16 + u, 2)], n_s.at[i], n_r.at[i], near, t
        )

    def m_copy(i, side=core):
        u = 16 + 8 * side + 2 * i
        return remote(nrm.at[pl.ds(u, 2)], nrm.at[pl.ds(u, 2)], m_s.at[i], m_r.at[i], d, sib)

    def part(k, owner, half):
        rows = shards[k][0].shape[0] // 2
        return shards[k][1].at[owner, pl.ds(pl.multiple_of(half * rows, 64), rows)]

    def wa_copy(k, owner=t):
        full = shards[k][1]
        return remote(full.at[owner], full.at[owner], wa_s.at[k], wa_r.at[k], d, sib)

    def wy_copy(k, owner=t):
        ref = part(k, owner, odd)
        return remote(ref, ref, wy_s.at[k], wy_r.at[k], d, across)

    def wx_copy(k, half=odd):
        ref = part(k, across, half)
        return remote(ref, ref, wx_s.at[k], wx_r.at[k], near, t)

    def w0_copy(k, owner=across):
        ref = part(k, owner, odd)
        return remote(ref, ref, w0_s.at[k], w0_r.at[k], d, sib)

    def w1_copy(k, owner=across):
        ref = part(k, owner, 1 - odd)
        return remote(ref, ref, w1_s.at[k], w1_r.at[k], d, sib)

    norm_quarter(0, 0)
    pl.semaphore_wait(barrier, 6)
    for i in range(4):
        for f in (1, 2):
            z_copy(f, i).start()
    lax.fori_loop(1, 4, norm_quarter, 0)
    n_copy(0).start()

    for copy in own_copies:
        copy.wait()
    for k in range(3):
        wa_copy(k).start()
    for c in range(3):
        wqkv[:, c * 128 : (c + 1) * 128] = wqkv_raw[c]

    def project_own(k, carry):
        rows = pl.ds(4 * k, 4)
        made = jnp.dot(
            nrm[rows].reshape(512, 512), wqkv[...], preferred_element_type=f32
        ).astype(bf16)
        query[rows] = made[:, :128].reshape(4, 128, 128)
        kv[rows] = made[:, 128:].reshape(4, 128, 256)
        return carry

    lax.fori_loop(0, 4, project_own, 0)

    def project(slot, quarter):
        rows = pl.ds(slot * 16 + 4 * quarter, 4)
        kv[rows] = (
            jnp.dot(nrm[rows].reshape(512, 512), wqkv[:, 128:], preferred_element_type=f32)
            .astype(bf16)
            .reshape(4, 128, 256)
        )

    def project_flows(quarter):
        lax.fori_loop(0, FLOWS, lambda f, c: (project(2 + f, quarter), c)[1], 0)

    def relay(i, carry):
        @pl.when(i < 4)
        def _():
            for f in (1, 2):
                z_copy(f, i).wait_recv()
            x_copy(i).start()
            for f in (1, 2):
                y_copy(f, i).start()
                a_copy(f, i).start()

        @pl.when(i < 3)
        def _():
            n_copy(i + 1).start()

        @pl.when((i > 0) & (i < 5))
        def _():
            n_copy(i - 1).wait_recv()
            m_copy(i - 1).start()
            x_copy(i - 1).wait_recv()
            y_copy(0, i - 1).start()
            a_copy(0, i - 1).start()

        @pl.when(i == 5)
        def _():
            for k in range(3):
                wy_copy(k).start()
            project_flows(t)
            project(1, 2 * core)
            project(1, 2 * core + 1)

        @pl.when(i > 1)
        def _():
            for f in range(FLOWS):
                y_copy(f, i - 2, across).wait_recv()
                b_copy(f, i - 2).start()

        return carry

    lax.fori_loop(0, 6, relay, 0)
    project_flows(across)
    for i in range(4):
        for f in range(FLOWS):
            a_copy(f, i, sib).wait_recv()
        m_copy(i, 1 - core).wait_recv()
    project_flows(sib)
    project(1, 2 - 2 * core)
    project(1, 3 - 2 * core)
    for i in range(4):
        for f in range(FLOWS):
            b_copy(f, i, corner).wait_recv()
    project_flows(corner)

    scale = 1.0 / math.sqrt(128)
    lane_entry = lax.broadcasted_iota(jnp.int32, (1, KMAX * NODE_BLK), 1) // NODE_BLK

    def place_of(b, j):
        block = neigh[b, j]
        away = lax.rem(lax.div(block, 8) - d + doms, doms)
        slot = jnp.where(away == 1, 1 + odd, 0)
        slot = jnp.where(away == doms - 1, 2 - odd, slot)
        slot = jnp.where(away == 2, 3, slot)
        slot = jnp.where(away == doms - 2, 4, slot)
        return slot * 16 + lax.rem(block, 8)

    def attend(b):
        firsts = [place_of(b, j) for j in range(KMAX)]
        made = []
        for s in range(2):
            q = query[s * 8 + b]
            scores = jnp.concatenate(
                [
                    lax.dot_general(
                        q, kv[first + s * 8, :, :128], (((1,), (1,)), ((), ())),
                        preferred_element_type=f32,
                    )
                    for first in firsts
                ],
                axis=1,
            )
            scores = jnp.where(lane_entry < live[b], scores, -1e30)
            top = jnp.max(scores, axis=1, keepdims=True)
            weights = jnp.exp((scores - top) * scale)
            whole = jnp.sum(weights, axis=1, keepdims=True)
            weights = weights.astype(bf16)
            mixed = jnp.zeros((NODE_BLK, 128), f32)
            for j, first in enumerate(firsts):
                mixed += jnp.dot(
                    weights[:, j * 128 : (j + 1) * 128], kv[first + s * 8, :, 128:],
                    preferred_element_type=f32,
                )
            made.append((mixed / whole).astype(bf16))
        return jnp.concatenate(made, axis=0)

    def h_copy(k, src_tp=t):
        owner = lax.rem(t + 1 + k // 2, 4)
        place = lax.rem(k, 2) * 256
        return remote(
            outgoing.at[k], heads.at[src_tp, pl.ds(place, 256)], h_s.at[k], h_r.at[k], d, owner
        )

    def attend_away(k, carry):
        for step, ready in ((2, (0, 1)), (4, (2,))):

            @pl.when(k == step)
            def _():
                for w in ready:
                    wy_copy(w, across).wait_recv()
                    wx_copy(w).start()
                    w0_copy(w).start()

        outgoing[k] = attend(lax.rem(2 * (t + 1) + k, 8))
        h_copy(k).start()
        return carry

    lax.fori_loop(0, 6, attend_away, 0)
    for w in range(2):
        wx_copy(w, 1 - odd).wait_recv()
        w1_copy(w).start()

    def attend_here(r, carry):
        heads[t, pl.ds(pl.multiple_of(r * 256, 256), 256)] = attend(2 * t + r)
        return carry

    lax.fori_loop(0, 2, attend_here, 0)

    wx_copy(2, 1 - odd).wait_recv()
    w1_copy(2).start()
    for k in range(6):
        h_copy(k, lax.rem(t + 3 - k // 2, 4)).wait_recv()
    for k in range(3):
        wa_copy(k, sib).wait_recv()
        w0_copy(k, corner).wait_recv()
        w1_copy(k, corner).wait_recv()

    def o_copy(k, r, owner=t):
        peer = lax.rem(t + 1 + k, 4)
        rows = pl.ds(pl.multiple_of(r * 256, 256), 256)
        return remote(
            cols.at[peer, rows], out.at[owner, rows], o_s.at[k, r], o_r.at[k, r], d, peer
        )

    def finish(r, carry):
        rows = pl.ds(pl.multiple_of(r * 256, 256), 256)
        attn = jnp.zeros((256, 512), f32)
        for h in range(HEADS):
            attn += (
                jnp.dot(heads[h, rows], wout_all[h], preferred_element_type=f32)
                .astype(bf16)
                .astype(f32)
            )
        after = []
        for s in range(2):
            after.append(
                state[s * 8 + 2 * t + r].astype(f32) + attn[s * 128 : (s + 1) * 128]
            )
            normed2[s * 128 : (s + 1) * 128] = layer_norm(
                after[s], gain[1, s : s + 1], shift[1, s : s + 1]
            ).astype(bf16)

        def hidden_group(g, total):
            pre = jnp.dot(normed2[...], wup_all[g], preferred_element_type=f32)
            hidden = (0.5 * pre * (1.0 + jnp.tanh(0.5 * pre))).astype(bf16)
            term = jnp.dot(hidden, wdown_all[g], preferred_element_type=f32)
            return total + term.astype(bf16).astype(f32)

        total = lax.fori_loop(0, 4, hidden_group, jnp.concatenate(after, axis=0))
        for j in range(4):
            cols[j, rows] = total[:, j * 128 : (j + 1) * 128].astype(bf16)
        for k in range(3):
            o_copy(k, r).start()
        out[t, rows] = cols[t, rows]
        return carry

    lax.fori_loop(0, 2, finish, 0)

    def drain(i, carry):
        for f in (1, 2):
            z_copy(f, i).wait_send()
        for f in range(FLOWS):
            y_copy(f, i).wait_send()
            a_copy(f, i).wait_send()
            b_copy(f, i).wait_send()
        x_copy(i).wait_send()
        n_copy(i).wait_send()
        m_copy(i).wait_send()
        return carry

    lax.fori_loop(0, 4, drain, 0)
    for k in range(3):
        for copy in (wy_copy, wa_copy, wx_copy, w0_copy, w1_copy):
            copy(k).wait_send()
    for k in range(6):
        h_copy(k).wait_send()
    for r in range(2):
        for k in range(3):
            o_copy(k, r, lax.rem(t + 3 - k, 4)).wait_recv()
            o_copy(k, r).wait_send()


def local(
    state, norm_gain, norm_shift, qkv_weight, out_weight, up_weight, down_weight, neighbours, counts
):
    samples, row_count, feat = state.shape
    per_dev = row_count // NODE_BLK
    bf16 = jnp.bfloat16
    dma = pltpu.SemaphoreType.DMA
    smem = pl.BlockSpec(memory_space=pltpu.SMEM)
    vmem = pl.BlockSpec(memory_space=pltpu.VMEM)
    anywhere = pl.BlockSpec(memory_space=pl.ANY)
    pairs = [dma((4,)), dma((4,))]
    for shape in [(2, 4)] + [(3, 4)] * 3 + [(4,)] * 3 + [(3,)] * 5 + [(6,), (3, 2)]:
        pairs += [dma(shape), dma(shape)]
    out = pl.pallas_call(
        layer_kernel,
        out_shape=jax.ShapeDtypeStruct((4, 512, 128), bf16),
        in_specs=[smem, smem, vmem, vmem] + [anywhere] * 5,
        out_specs=vmem,
        scratch_shapes=[
            pltpu.VMEM((16, 128, 512), bf16),
            pltpu.VMEM((3, 512, 128), bf16),
            pltpu.VMEM((512, 384), bf16),
            pltpu.VMEM((80, 128, 512), bf16),
            pltpu.VMEM((80, 128, 256), bf16),
            pltpu.VMEM((16, 128, 128), bf16),
            pltpu.VMEM((4, 512, 128), bf16),
            pltpu.VMEM((6, 256, 128), bf16),
            pltpu.VMEM((4, 128, 512), bf16),
            pltpu.VMEM((4, 512, 512), bf16),
            pltpu.VMEM((4, 512, 512), bf16),
            pltpu.VMEM((256, 512), bf16),
            pltpu.VMEM((4, 512, 128), bf16),
        ]
        + pairs,
        compiler_params=pltpu.CompilerParams(
            collective_id=0, has_side_effects=True, vmem_limit_bytes=62 * 2**20
        ),
    )(
        neighbours,
        counts,
        norm_gain,
        norm_shift,
        state.reshape(samples * per_dev, NODE_BLK, feat),
        jnp.transpose(qkv_weight, (1, 0, 2)),
        out_weight,
        up_weight,
        down_weight,
    )
    out = out.reshape(per_dev, samples, NODE_BLK, 128)
    return jnp.transpose(out, (1, 0, 2, 3)).reshape(samples, row_count, 128)


def solution(mesh):
    placed = (
        P(None, "dom", None),
        P(),
        P(),
        P(None, None, "tp"),
        P("tp", None),
        P(None, "tp"),
        P("tp", None),
        P("dom", None),
        P("dom"),
    )
    return jax.shard_map(
        local, mesh=mesh, in_specs=placed, out_specs=P(None, "dom", "tp"), check_vma=False
    )
```

time: 104 us -> 86.8 us (0.83)
  Pallas kernels: 95.3 us -> 84.6 us
  local copies, waits for them, and re-layouts: 7.25 us -> 1.89 us
    pallas_call x1, Pallas kernels: 95.3 us -> 84.6 us  [local(): pl.pallas_call(layer_kernel, out_shape=jax.ShapeDtypeStruct((4, 512, 128)...]
    unnamed x9 -> x0, local copies, waits for them, and re-layouts: 4.8 us -> none
    reshape x3 -> x0, local copies, waits for them, and re-layouts: 1.62 us -> none  [the longest x1 0.7 us: local(): norm_gain.reshape(2, 2, 1, feat)]
    transpose x1, local copies, waits for them, and re-layouts: 0.83 us -> 1.89 us  [local(): return jnp.transpose(out, (1, 0, 2, 3)).reshape(samples, row_count, 128)]
where the time goes in v2:
time: 86.8 us; the launch traced here: 86.5 us
  Pallas kernels  84.6 us (97%)
  local copies, waits for them, and re-layouts  1.89 us (2%)
    pallas_call x1, Pallas kernels, local(): pl.pallas_call(layer_kernel, out_shape=jax.ShapeDtypeStruct((4, 512, 128)...  84.6 us
    transpose x1, local copies, waits for them, and re-layouts, local(): return jnp.transpose(out, (1, 0, 2, 3)).reshape(samples, row_count, 128)  1.89 us

profile of v2, /device:TPU:1, one launch (start us, length us, event | category | flops | bytes accessed | tf_op | source)
XLA Modules:
  0.0 86.5 jit_solution(13537269742820464476)
XLA Ops:
  0.0 84.6 %shard_map.91 = bf16[4,512,128]{2,1,0:T(8,128)(2,1)} custom-call(s32[8,8]{1,0:T(8,128)} %neigh.1, s32[8]{0:T(128)} %live.1, f32[2,2,512]{2,1,0:T(2,128)} %gain.1, f32[2,2,512]{2,1,0:T(2,128)} %shift.1, bf16[16,128,512]{2,1,0:T(8,128)(2,1)} %bitcast.6, bf16[3,512,128]{2,1,0:T(8,128)(2,1)} %bitcast.8, bf16[128,512]{1,0:T(8,128)(2,1)} %wout_in.1, ...), custom_call_target="tpu_custom_call" | custom-call | tf_op jit(solution)/shard_map/pallas_call | solution.py:391
  84.6 1.9 %copy.10 = bf16[2,8,128,128]{3,2,1,0:T(8,128)(2,1)} copy(bf16[2,8,128,128]{3,2,0,1:T(8,128)(2,1)} %bitcast.7) | data formatting | bytes 1048576 | tf_op jit(solution)/shard_map/transpose | solution.py:427

commit v3 on v2

v3 whole, which is shorter than its diff:
```python
import math

import jax
import jax.numpy as jnp
from jax import lax
from jax.experimental import pallas as pl
from jax.experimental.pallas import tpu as pltpu
from jax.sharding import PartitionSpec as P

HEADS = 4
NODE_BLK = 128
KMAX = 8


def layer_norm(values, gain_row, shift_row):
    row_mean = jnp.mean(values, axis=-1, keepdims=True)
    centred = values - row_mean
    spread = jnp.mean(centred * centred, axis=-1, keepdims=True)
    return centred * lax.rsqrt(spread + 1e-05) * gain_row + shift_row


def layer_kernel(
    neigh, live, gain, shift, state_in, wqkv_in, wout_in, wup_in, wdown_in, out,
    state, wqkv_raw, wqkv, nrm, kv, query, heads, outgoing, wout_all, wup_all, wdown_all, normed2,
    cols, c_state, c_w,
    z_s, z_r, y_s, y_r, a_s, a_r, b_s, b_r, x_s, x_r, n_s, n_r, m_s, m_r,
    wy_s, wy_r, wa_s, wa_r, wx_s, wx_r, w0_s, w0_r, w1_s, w1_r, h_s, h_r, o_s, o_r,
):
    d = lax.axis_index("dom")
    t = lax.axis_index("tp")
    doms = lax.axis_size("dom")
    odd = lax.rem(d, 2)
    near = d + 1 - 2 * odd
    plus = lax.rem(d + 2, doms)
    minus = lax.rem(d + doms - 2, doms)
    core = lax.rem(t, 2)
    sib = t + 1 - 2 * core
    across = lax.rem(t + 2, 4)
    corner = lax.rem(sib + 2, 4)
    f32 = jnp.float32
    bf16 = jnp.bfloat16

    def remote(src, dst, send, recv, dd, tt):
        return pltpu.make_async_remote_copy(
            src_ref=src, dst_ref=dst, send_sem=send, recv_sem=recv, device_id=(dd, tt),
            device_id_type=pl.DeviceIdType.MESH,
        )

    barrier = pltpu.get_barrier_semaphore()
    for partner in [(near, t), (plus, t), (minus, t), (d, sib), (d, across), (d, corner)]:
        pl.semaphore_signal(
            barrier, inc=1, device_id=partner, device_id_type=pl.DeviceIdType.MESH
        )

    def state_copy(s):
        rows = pl.ds(8 * s, 8)
        return pltpu.make_async_copy(state_in.at[rows], state.at[rows], c_state.at[s])

    shards = ((wout_in, wout_all), (wup_in, wup_all), (wdown_in, wdown_all))
    own_copies = [pltpu.make_async_copy(wqkv_in, wqkv_raw, c_w.at[3])] + [
        pltpu.make_async_copy(shard, full.at[t], c_w.at[k])
        for k, (shard, full) in enumerate(shards)
    ]
    for s in range(2):
        state_copy(s).start()
    for copy in own_copies:
        copy.start()

    def norm_units(s, first, count, around=8):
        def norm_one(i, inner):
            u = 8 * s + lax.rem(first + i, around)
            nrm[u] = layer_norm(
                state[u].astype(f32), gain[0, s : s + 1], shift[0, s : s + 1]
            ).astype(bf16)
            return inner

        lax.fori_loop(0, count, norm_one, 0)

    def unit(rank, j):
        side = lax.div(rank, 2)
        shared = 4 + 2 * lax.rem(rank, 2)
        return (rank, shared + side, shared + 1 - side)[j]

    def z_copy(f, s, j):
        u = 8 * s + unit(t, j)
        return remote(
            nrm.at[u], nrm.at[(2 + f) * 16 + u], z_s.at[f - 1, 3 * s + j],
            z_r.at[f - 1, 3 * s + j], (minus, plus)[f - 1], t,
        )

    def x_copy(s, j):
        u = 8 * s + unit(t, j)
        k = 2 * s + j
        return remote(
            nrm.at[(3 + odd) * 16 + u], nrm.at[2 * 16 + u], x_s.at[k], x_r.at[k], near, t
        )

    def y_copy(f, s, j, owner=t):
        u = (2 + f) * 16 + 8 * s + unit(owner, j)
        k = 2 * s + j
        return remote(nrm.at[u], nrm.at[u], y_s.at[f, k], y_r.at[f, k], d, across)

    def a_copy(f, s, j, owner=t):
        u = (2 + f) * 16 + 8 * s + unit(owner, j)
        k = 3 * s + j
        return remote(nrm.at[u], nrm.at[u], a_s.at[f, k], a_r.at[f, k], d, sib)

    def b_copy(f, s, j, owner=across):
        u = (2 + f) * 16 + 8 * s + unit(owner, j)
        k = 2 * s + j
        return remote(nrm.at[u], nrm.at[u], b_s.at[f, k], b_r.at[f, k], d, sib)

    def n_copy(i):
        u = 8 * (i // 2) + 4 * core + 2 * (i % 2)
        return remote(
            nrm.at[pl.ds(u, 2)], nrm.at[pl.ds(16 + u, 2)], n_s.at[i], n_r.at[i], near, t
        )

    def m_copy(i, side=core):
        u = 16 + 8 * (i // 2) + 4 * side + 2 * (i % 2)
        return remote(nrm.at[pl.ds(u, 2)], nrm.at[pl.ds(u, 2)], m_s.at[i], m_r.at[i], d, sib)

    def part(k, owner, half):
        rows = shards[k][0].shape[0] // 2
        return shards[k][1].at[owner, pl.ds(pl.multiple_of(half * rows, 64), rows)]

    def wa_copy(k, owner=t):
        full = shards[k][1]
        return remote(full.at[owner], full.at[owner], wa_s.at[k], wa_r.at[k], d, sib)

    def wy_copy(k, owner=t):
        ref = part(k, owner, odd)
        return remote(ref, ref, wy_s.at[k], wy_r.at[k], d, across)

    def wx_copy(k, half=odd):
        ref = part(k, across, half)
        return remote(ref, ref, wx_s.at[k], wx_r.at[k], near, t)

    def w0_copy(k, owner=across):
        ref = part(k, owner, odd)
        return remote(ref, ref, w0_s.at[k], w0_r.at[k], d, sib)

    def w1_copy(k, owner=across):
        ref = part(k, owner, 1 - odd)
        return remote(ref, ref, w1_s.at[k], w1_r.at[k], d, sib)

    state_copy(0).wait()
    norm_units(0, t, 1)
    norm_units(0, 4 + 2 * core, 2)
    pl.semaphore_wait(barrier, 6)
    for j in range(3):
        for f in (1, 2):
            z_copy(f, 0, j).start()
    norm_units(0, t + 1, 3, 4)
    norm_units(0, 6 - 2 * core, 2)
    n_copy(0).start()
    n_copy(1).start()
    for copy in own_copies:
        copy.wait()
    for k in range(2):
        wy_copy(k).start()
    state_copy(1).wait()
    norm_units(1, 0, 8)
    for j in range(3):
        for f in (1, 2):
            z_copy(f, 1, j).start()
    for k in range(3):
        wa_copy(k).start()
    for c in range(3):
        wqkv[:, c * 128 : (c + 1) * 128] = wqkv_raw[c]

    def project_own(k, carry):
        rows = pl.ds(4 * k, 4)
        made = jnp.dot(
            nrm[rows].reshape(512, 512), wqkv[...], preferred_element_type=f32
        ).astype(bf16)
        query[rows] = made[:, :128].reshape(4, 128, 128)
        kv[rows] = made[:, 128:].reshape(4, 128, 256)
        return carry

    lax.fori_loop(0, 4, project_own, 0)

    def project(slot, s, half):
        rows = pl.ds(slot * 16 + 8 * s + 4 * half, 4)
        kv[rows] = (
            jnp.dot(nrm[rows].reshape(512, 512), wqkv[:, 128:], preferred_element_type=f32)
            .astype(bf16)
            .reshape(4, 128, 256)
        )

    def project_slots(s, half, low, high):
        lax.fori_loop(low, high, lambda slot, c: (project(slot, s, half), c)[1], 0)

    def pull(s, j):
        for f in (1, 2):
            z_copy(f, s, j).wait_recv()
        if j < 2:
            x_copy(s, j).start()
        for f in (1, 2):
            if j == 0:
                y_copy(f, s, 0).start()
            a_copy(f, s, j).start()

    def pull_diagonal(s, j):
        x_copy(s, j).wait_recv()
        y_copy(0, s, j).start()
        a_copy(0, s, j).start()

    def pull_near(i):
        n_copy(i).wait_recv()
        m_copy(i).start()

    crossed = ((1, 0), (2, 0), (0, 0), (0, 1))

    def pass_on(s):
        for f, j in crossed:
            y_copy(f, s, j, across).wait_recv()
            b_copy(f, s, j).start()

    def take_direct(s):
        for j in range(3):
            for f in (1, 2):
                a_copy(f, s, j, sib).wait_recv()
        for i in (2 * s, 2 * s + 1):
            m_copy(i, 1 - core).wait_recv()
        project_slots(s, 0, 1, 2)
        project_slots(s, 1, 1, 2)
        project_slots(s, 1, 3, 5)

    def take_rest(s):
        for j in range(2):
            a_copy(0, s, j, sib).wait_recv()
        for f, j in crossed:
            b_copy(f, s, j, corner).wait_recv()
        project_slots(s, 0, 2, 5)
        project_slots(s, 1, 2, 3)

    scale = 1.0 / math.sqrt(128)
    lane_entry = lax.broadcasted_iota(jnp.int32, (1, KMAX * NODE_BLK), 1) // NODE_BLK

    def place_of(b, j):
        block = neigh[b, j]
        away = lax.rem(lax.div(block, 8) - d + doms, doms)
        slot = jnp.where(away == 1, 1 + odd, 0)
        slot = jnp.where(away == doms - 1, 2 - odd, slot)
        slot = jnp.where(away == 2, 3, slot)
        slot = jnp.where(away == doms - 2, 4, slot)
        return slot * 16 + lax.rem(block, 8)

    def attend(b, s):
        places = [place_of(b, j) + s * 8 for j in range(KMAX)]
        keys = jnp.concatenate([kv[place, :, :128] for place in places], axis=0)
        values = jnp.concatenate([kv[place, :, 128:] for place in places], axis=0)
        scores = lax.dot_general(
            query[s * 8 + b], keys, (((1,), (1,)), ((), ())), preferred_element_type=f32
        )
        scores = jnp.where(lane_entry < live[b], scores, -1e30)
        top = jnp.max(scores, axis=1, keepdims=True)
        weights = jnp.exp((scores - top) * scale)
        whole = jnp.sum(weights, axis=1, keepdims=True)
        mixed = jnp.dot(weights.astype(bf16), values, preferred_element_type=f32)
        return (mixed / whole).astype(bf16)

    def attend_pair(owner, s):
        return jnp.concatenate([attend(2 * owner + r, s) for r in range(2)], axis=0)

    def h_copy(k, s, src_tp=t):
        owner = lax.rem(t + 1 + k, 4)
        return remote(
            outgoing.at[3 * s + k], heads.at[src_tp, pl.ds(s * 256, 256)], h_s.at[3 * s + k],
            h_r.at[3 * s + k], d, owner,
        )

    def attend_away(s, low, high):
        def one(k, carry):
            outgoing[3 * s + k] = attend_pair(lax.rem(t + 1 + k, 4), s)
            h_copy(k, s).start()
            return carry

        lax.fori_loop(low, high, one, 0)

    def attend_here(s):
        heads[t, s * 256 : (s + 1) * 256] = attend_pair(t, s)

    def spread(ready):
        for w in ready:
            wy_copy(w, across).wait_recv()
            wx_copy(w).start()
            w0_copy(w).start()

    for j in range(3):
        pull(0, j)
    wy_copy(2).start()
    pull_diagonal(0, 0)
    pull_diagonal(0, 1)
    n_copy(2).start()
    pull_near(0)
    pull_near(1)
    pull(1, 0)
    n_copy(3).start()
    take_direct(0)
    pass_on(0)
    take_rest(0)
    spread((0, 1))
    attend_away(0, 0, 1)
    pull(1, 1)
    attend_away(0, 1, 3)
    pull_diagonal(1, 0)
    spread((2,))
    attend_here(0)
    pull(1, 2)
    pull_diagonal(1, 1)
    pull_near(2)
    pull_near(3)
    take_direct(1)
    pass_on(1)
    take_rest(1)
    attend_away(1, 0, 3)
    for w in range(3):
        wx_copy(w, 1 - odd).wait_recv()
        w1_copy(w).start()
    attend_here(1)
    for k in range(3):
        wa_copy(k, sib).wait_recv()
        w0_copy(k, corner).wait_recv()
        w1_copy(k, corner).wait_recv()

    def o_copy(k, s, owner=t):
        peer = lax.rem(t + 1 + k, 4)
        return remote(
            cols.at[peer, pl.ds(s * 256, 256)],
            out.at[s, pl.ds(pl.multiple_of(owner * 256, 256), 256)],
            o_s.at[k, s], o_r.at[k, s], d, peer,
        )

    def finish(s):
        for k in range(3):
            h_copy(k, s, lax.rem(t + 3 - k, 4)).wait_recv()
        rows = slice(s * 256, (s + 1) * 256)
        attn = jnp.zeros((256, 512), f32)
        for h in range(HEADS):
            attn += (
                jnp.dot(heads[h, rows], wout_all[h], preferred_element_type=f32)
                .astype(bf16)
                .astype(f32)
            )
        after = state[pl.ds(8 * s + 2 * t, 2)].reshape(256, 512).astype(f32) + attn
        normed2[...] = layer_norm(after, gain[1, s : s + 1], shift[1, s : s + 1]).astype(bf16)

        def hidden_group(g, total):
            pre = jnp.dot(normed2[...], wup_all[g], preferred_element_type=f32)
            hidden = (0.5 * pre * (1.0 + jnp.tanh(0.5 * pre))).astype(bf16)
            term = jnp.dot(hidden, wdown_all[g], preferred_element_type=f32)
            return total + term.astype(bf16).astype(f32)

        total = lax.fori_loop(0, 4, hidden_group, after)
        for j in range(4):
            cols[j, rows] = total[:, j * 128 : (j + 1) * 128].astype(bf16)
        for k in range(3):
            o_copy(k, s).start()
        out[s, pl.ds(pl.multiple_of(t * 256, 256), 256)] = cols[t, rows]

    for s in range(2):
        finish(s)

    for s in range(2):
        for j in range(3):
            for f in (1, 2):
                z_copy(f, s, j).wait_send()
                a_copy(f, s, j).wait_send()
        for j in range(2):
            x_copy(s, j).wait_send()
            a_copy(0, s, j).wait_send()
        for f, j in crossed:
            y_copy(f, s, j).wait_send()
            b_copy(f, s, j).wait_send()
    for i in range(4):
        n_copy(i).wait_send()
        m_copy(i).wait_send()
    for k in range(3):
        for copy in (wy_copy, wa_copy, wx_copy, w0_copy, w1_copy):
            copy(k).wait_send()
        for s in range(2):
            h_copy(k, s).wait_send()
    for s in range(2):
        for k in range(3):
            o_copy(k, s, lax.rem(t + 3 - k, 4)).wait_recv()
            o_copy(k, s).wait_send()


def local(
    state, norm_gain, norm_shift, qkv_weight, out_weight, up_weight, down_weight, neighbours, counts
):
    samples, row_count, feat = state.shape
    per_dev = row_count // NODE_BLK
    bf16 = jnp.bfloat16
    dma = pltpu.SemaphoreType.DMA
    smem = pl.BlockSpec(memory_space=pltpu.SMEM)
    vmem = pl.BlockSpec(memory_space=pltpu.VMEM)
    anywhere = pl.BlockSpec(memory_space=pl.ANY)
    pairs = [dma((2,)), dma((4,))]
    for shape in [(2, 6), (3, 4), (3, 6), (3, 4)] + [(4,)] * 3 + [(3,)] * 5 + [(6,), (3, 2)]:
        pairs += [dma(shape), dma(shape)]
    return pl.pallas_call(
        layer_kernel,
        out_shape=jax.ShapeDtypeStruct((samples, row_count, 128), bf16),
        in_specs=[smem, smem, vmem, vmem] + [anywhere] * 5,
        out_specs=vmem,
        scratch_shapes=[
            pltpu.VMEM((16, 128, 512), bf16),
            pltpu.VMEM((3, 512, 128), bf16),
            pltpu.VMEM((512, 384), bf16),
            pltpu.VMEM((80, 128, 512), bf16),
            pltpu.VMEM((80, 128, 256), bf16),
            pltpu.VMEM((16, 128, 128), bf16),
            pltpu.VMEM((4, 512, 128), bf16),
            pltpu.VMEM((6, 256, 128), bf16),
            pltpu.VMEM((4, 128, 512), bf16),
            pltpu.VMEM((4, 512, 512), bf16),
            pltpu.VMEM((4, 512, 512), bf16),
            pltpu.VMEM((256, 512), bf16),
            pltpu.VMEM((4, 512, 128), bf16),
        ]
        + pairs,
        compiler_params=pltpu.CompilerParams(
            collective_id=0, has_side_effects=True, vmem_limit_bytes=62 * 2**20
        ),
    )(
        neighbours,
        counts,
        norm_gain,
        norm_shift,
        state.reshape(samples * per_dev, NODE_BLK, feat),
        jnp.transpose(qkv_weight, (1, 0, 2)),
        out_weight,
        up_weight,
        down_weight,
    )


def solution(mesh):
    placed = (
        P(None, "dom", None),
        P(),
        P(),
        P(None, None, "tp"),
        P("tp", None),
        P(None, "tp"),
        P("tp", None),
        P("dom", None),
        P("dom"),
    )
    return jax.shard_map(
        local, mesh=mesh, in_specs=placed, out_specs=P(None, "dom", "tp"), check_vma=False
    )
```

time: 86.8 us -> 81.3 us (0.937)
  Pallas kernels: 84.6 us -> 79.2 us
    pallas_call x1, Pallas kernels: 84.6 us -> 79.2 us  [local(): pl.pallas_call(layer_kernel, out_shape=jax.ShapeDtypeStruct((samples, row...]
    transpose x1 -> x0, local copies, waits for them, and re-layouts: 1.89 us -> none  [local(): return jnp.transpose(out, (1, 0, 2, 3)).reshape(samples, row_count, 128)]
    unnamed x0 -> x1, local copies, waits for them, and re-layouts: none -> 1.87 us
where the time goes in v3:
time: 81.3 us; the launch traced here: 81 us
  Pallas kernels  79.2 us (97%)
  local copies, waits for them, and re-layouts  1.87 us (2%)
    pallas_call x1, Pallas kernels, local(): pl.pallas_call(layer_kernel, out_shape=jax.ShapeDtypeStruct((samples, row...  79.2 us
    unnamed x1, local copies, waits for them, and re-layouts  1.87 us

profile of v3, /device:TPU:1, one launch (start us, length us, event | category | flops | bytes accessed | tf_op | source)
XLA Modules:
  0.0 81.0 jit_solution(494103757981892292)
XLA Ops:
  0.0 79.2 %shard_map.91 = bf16[2,1024,128]{2,1,0:T(8,128)(2,1)} custom-call(s32[8,8]{1,0:T(8,128)} %neigh.1, s32[8]{0:T(128)} %live.1, f32[2,2,512]{2,1,0:T(2,128)} %gain.1, f32[2,2,512]{2,1,0:T(2,128)} %shift.1, bf16[16,128,512]{2,1,0:T(8,128)(2,1)} %bitcast.2, bf16[3,512,128]{2,1,0:T(8,128)(2,1)} %bitcast.3, bf16[128,512]{1,0:T(8,128)(2,1)} %wout_in.1, ...), custom_call_target="tpu_custom_call" | custom-call | tf_op jit(solution)/shard_map/pallas_call | solution.py:404
  79.2 1.9 %copy.11 = bf16[2,1024,128]{2,1,0:T(8,128)(2,1)} copy(bf16[2,1024,128]{2,1,0:T(8,128)(2,1)} %shard_map.91) | data formatting | bytes 1048576

commit v4 on v3

--- a/solution.py
+++ b/solution.py
@@ -121,6 +121,8 @@
         return remote(nrm.at[pl.ds(u, 2)], nrm.at[pl.ds(u, 2)], m_s.at[i], m_r.at[i], d, sib)
 
     def part(k, owner, half):
+        if k == 2:
+            return wdown_all.at[owner]
         rows = shards[k][0].shape[0] // 2
         return shards[k][1].at[owner, pl.ds(pl.multiple_of(half * rows, 64), rows)]
 
@@ -161,9 +163,6 @@
         wy_copy(k).start()
     state_copy(1).wait()
     norm_units(1, 0, 8)
-    for j in range(3):
-        for f in (1, 2):
-            z_copy(f, 1, j).start()
     for k in range(3):
         wa_copy(k).start()
     for c in range(3):
@@ -194,6 +193,8 @@
     def pull(s, j):
         for f in (1, 2):
             z_copy(f, s, j).wait_recv()
+            if s == 0:
+                z_copy(f, 1, j).start()
         if j < 2:
             x_copy(s, j).start()
         for f in (1, 2):
@@ -290,39 +291,42 @@
 
     for j in range(3):
         pull(0, j)
-    wy_copy(2).start()
     pull_diagonal(0, 0)
     pull_diagonal(0, 1)
     n_copy(2).start()
     pull_near(0)
     pull_near(1)
+    take_direct(0)
+    pass_on(0)
     pull(1, 0)
     n_copy(3).start()
-    take_direct(0)
-    pass_on(0)
     take_rest(0)
-    spread((0, 1))
     attend_away(0, 0, 1)
     pull(1, 1)
-    attend_away(0, 1, 3)
+    attend_away(0, 1, 2)
     pull_diagonal(1, 0)
-    spread((2,))
-    attend_here(0)
+    attend_away(0, 2, 3)
     pull(1, 2)
     pull_diagonal(1, 1)
+    wy_copy(2).start()
+    spread((0, 1))
     pull_near(2)
     pull_near(3)
+    attend_here(0)
     take_direct(1)
     pass_on(1)
     take_rest(1)
     attend_away(1, 0, 3)
-    for w in range(3):
+    for w in range(2):
         wx_copy(w, 1 - odd).wait_recv()
         w1_copy(w).start()
+    wy_copy(2, across).wait_recv()
+    w0_copy(2).start()
     attend_here(1)
     for k in range(3):
         wa_copy(k, sib).wait_recv()
         w0_copy(k, corner).wait_recv()
+    for k in range(2):
         w1_copy(k, corner).wait_recv()
 
     def o_copy(k, s, owner=t):
@@ -378,7 +382,7 @@
         n_copy(i).wait_send()
         m_copy(i).wait_send()
     for k in range(3):
-        for copy in (wy_copy, wa_copy, wx_copy, w0_copy, w1_copy):
+        for copy in (wy_copy, wa_copy, w0_copy) + ((wx_copy, w1_copy) if k < 2 else ()):
             copy(k).wait_send()
         for s in range(2):
             h_copy(k, s).wait_send()

time: 81.3 us -> 76.1 us (0.936)
  Pallas kernels: 79.2 us -> 74 us
    pallas_call x1, Pallas kernels: 79.2 us -> 74 us  [local(): pl.pallas_call(layer_kernel, out_shape=jax.ShapeDtypeStruct((samples, row...]
where the time goes in v4:
time: 76.1 us; the launch traced here: 75.9 us
  Pallas kernels  74 us (97%)
  local copies, waits for them, and re-layouts  1.87 us (2%)
    pallas_call x1, Pallas kernels, local(): pl.pallas_call(layer_kernel, out_shape=jax.ShapeDtypeStruct((samples, row...  74 us
    unnamed x1, local copies, waits for them, and re-layouts  1.87 us

profile of v4, /device:TPU:1, one launch (start us, length us, event | category | flops | bytes accessed | tf_op | source)
XLA Modules:
  0.0 75.9 jit_solution(12566270932472216994)
XLA Ops:
  0.0 74.0 %shard_map.91 = bf16[2,1024,128]{2,1,0:T(8,128)(2,1)} custom-call(s32[8,8]{1,0:T(8,128)} %neigh.1, s32[8]{0:T(128)} %live.1, f32[2,2,512]{2,1,0:T(2,128)} %gain.1, f32[2,2,512]{2,1,0:T(2,128)} %shift.1, bf16[16,128,512]{2,1,0:T(8,128)(2,1)} %bitcast.2, bf16[3,512,128]{2,1,0:T(8,128)(2,1)} %bitcast.3, bf16[128,512]{1,0:T(8,128)(2,1)} %wout_in.1, ...), custom_call_target="tpu_custom_call" | custom-call | tf_op jit(solution)/shard_map/pallas_call | solution.py:408
  74.0 1.9 %copy.11 = bf16[2,1024,128]{2,1,0:T(8,128)(2,1)} copy(bf16[2,1024,128]{2,1,0:T(8,128)(2,1)} %shard_map.91) | data formatting | bytes 1048576

commit v5 on v4

--- a/solution.py
+++ b/solution.py
@@ -177,7 +177,6 @@
         kv[rows] = made[:, 128:].reshape(4, 128, 256)
         return carry
 
-    lax.fori_loop(0, 4, project_own, 0)
 
     def project(slot, s, half):
         rows = pl.ds(slot * 16 + 8 * s + 4 * half, 4)
@@ -236,7 +235,7 @@
         project_slots(s, 0, 2, 5)
         project_slots(s, 1, 2, 3)
 
-    scale = 1.0 / math.sqrt(128)
+    scale = math.log2(math.e) / math.sqrt(128)
     lane_entry = lax.broadcasted_iota(jnp.int32, (1, KMAX * NODE_BLK), 1) // NODE_BLK
 
     def place_of(b, j):
@@ -252,15 +251,15 @@
         places = [place_of(b, j) + s * 8 for j in range(KMAX)]
         keys = jnp.concatenate([kv[place, :, :128] for place in places], axis=0)
         values = jnp.concatenate([kv[place, :, 128:] for place in places], axis=0)
+        values = jnp.concatenate([values, jnp.ones_like(values)], axis=1)
         scores = lax.dot_general(
             query[s * 8 + b], keys, (((1,), (1,)), ((), ())), preferred_element_type=f32
         )
         scores = jnp.where(lane_entry < live[b], scores, -1e30)
         top = jnp.max(scores, axis=1, keepdims=True)
-        weights = jnp.exp((scores - top) * scale)
-        whole = jnp.sum(weights, axis=1, keepdims=True)
-        mixed = jnp.dot(weights.astype(bf16), values, preferred_element_type=f32)
-        return (mixed / whole).astype(bf16)
+        weights = jnp.exp2((scores - top) * scale).astype(bf16)
+        mixed = jnp.dot(weights, values, preferred_element_type=f32)
+        return (mixed[:, :128] / mixed[:, 128:]).astype(bf16)
 
     def attend_pair(owner, s):
         return jnp.concatenate([attend(2 * owner + r, s) for r in range(2)], axis=0)
@@ -291,6 +290,8 @@
 
     for j in range(3):
         pull(0, j)
+        if j == 1:
+            lax.fori_loop(0, 4, project_own, 0)
     pull_diagonal(0, 0)
     pull_diagonal(0, 1)
     n_copy(2).start()
@@ -357,7 +358,7 @@
             term = jnp.dot(hidden, wdown_all[g], preferred_element_type=f32)
             return total + term.astype(bf16).astype(f32)
 
-        total = lax.fori_loop(0, 4, hidden_group, after)
+        total = lax.fori_loop(0, 4, hidden_group, after, unroll=True)
         for j in range(4):
             cols[j, rows] = total[:, j * 128 : (j + 1) * 128].astype(bf16)
         for k in range(3):

time: 76.1 us -> 74.6 us (0.980)
  Pallas kernels: 74 us -> 72.5 us
    pallas_call x1, Pallas kernels: 74 us -> 72.5 us  [local(): pl.pallas_call(layer_kernel, out_shape=jax.ShapeDtypeStruct((samples, row...]
where the time goes in v5:
time: 74.6 us; the launch traced here: 74.4 us
  Pallas kernels  72.5 us (97%)
  local copies, waits for them, and re-layouts  1.87 us (3%)
    pallas_call x1, Pallas kernels, local(): pl.pallas_call(layer_kernel, out_shape=jax.ShapeDtypeStruct((samples, row...  72.5 us
    unnamed x1, local copies, waits for them, and re-layouts  1.87 us

profile of v5, /device:TPU:1, one launch (start us, length us, event | category | flops | bytes accessed | tf_op | source)
XLA Modules:
  0.0 74.4 jit_solution(6475821865185079120)
XLA Ops:
  0.0 72.5 %shard_map.91 = bf16[2,1024,128]{2,1,0:T(8,128)(2,1)} custom-call(s32[8,8]{1,0:T(8,128)} %neigh.1, s32[8]{0:T(128)} %live.1, f32[2,2,512]{2,1,0:T(2,128)} %gain.1, f32[2,2,512]{2,1,0:T(2,128)} %shift.1, bf16[16,128,512]{2,1,0:T(8,128)(2,1)} %bitcast.2, bf16[3,512,128]{2,1,0:T(8,128)(2,1)} %bitcast.3, bf16[128,512]{1,0:T(8,128)(2,1)} %wout_in.1, ...), custom_call_target="tpu_custom_call" | custom-call | tf_op jit(solution)/shard_map/pallas_call | solution.py:409
  72.5 1.9 %copy.11 = bf16[2,1024,128]{2,1,0:T(8,128)(2,1)} copy(bf16[2,1024,128]{2,1,0:T(8,128)(2,1)} %shard_map.91) | data formatting | bytes 1048576

commit v6 on v5

--- a/solution.py
+++ b/solution.py
@@ -10,6 +10,7 @@
 HEADS = 4
 NODE_BLK = 128
 KMAX = 8
+SLOTS = (2, 3, 4, 1)
 
 
 def layer_norm(values, gain_row, shift_row):
@@ -23,7 +24,7 @@
     neigh, live, gain, shift, state_in, wqkv_in, wout_in, wup_in, wdown_in, out,
     state, wqkv_raw, wqkv, nrm, kv, query, heads, outgoing, wout_all, wup_all, wdown_all, normed2,
     cols, c_state, c_w,
-    z_s, z_r, y_s, y_r, a_s, a_r, b_s, b_r, x_s, x_r, n_s, n_r, m_s, m_r,
+    z_s, z_r, y_s, y_r, a_s, a_r, b_s, b_r, x_s, x_r, n_s, n_r,
     wy_s, wy_r, wa_s, wa_r, wx_s, wx_r, w0_s, w0_r, w1_s, w1_r, h_s, h_r, o_s, o_r,
 ):
     d = lax.axis_index("dom")
@@ -96,29 +97,24 @@
         )
 
     def y_copy(f, s, j, owner=t):
-        u = (2 + f) * 16 + 8 * s + unit(owner, j)
+        u = SLOTS[f] * 16 + 8 * s + unit(owner, j)
         k = 2 * s + j
         return remote(nrm.at[u], nrm.at[u], y_s.at[f, k], y_r.at[f, k], d, across)
 
     def a_copy(f, s, j, owner=t):
-        u = (2 + f) * 16 + 8 * s + unit(owner, j)
+        u = SLOTS[f] * 16 + 8 * s + unit(owner, j)
         k = 3 * s + j
         return remote(nrm.at[u], nrm.at[u], a_s.at[f, k], a_r.at[f, k], d, sib)
 
     def b_copy(f, s, j, owner=across):
-        u = (2 + f) * 16 + 8 * s + unit(owner, j)
+        u = SLOTS[f] * 16 + 8 * s + unit(owner, j)
         k = 2 * s + j
         return remote(nrm.at[u], nrm.at[u], b_s.at[f, k], b_r.at[f, k], d, sib)
 
-    def n_copy(i):
-        u = 8 * (i // 2) + 4 * core + 2 * (i % 2)
-        return remote(
-            nrm.at[pl.ds(u, 2)], nrm.at[pl.ds(16 + u, 2)], n_s.at[i], n_r.at[i], near, t
-        )
-
-    def m_copy(i, side=core):
-        u = 16 + 8 * (i // 2) + 4 * side + 2 * (i % 2)
-        return remote(nrm.at[pl.ds(u, 2)], nrm.at[pl.ds(u, 2)], m_s.at[i], m_r.at[i], d, sib)
+    def n_copy(s, j):
+        u = 8 * s + unit(t, j)
+        k = 3 * s + j
+        return remote(nrm.at[u], nrm.at[16 + u], n_s.at[k], n_r.at[k], near, t)
 
     def part(k, owner, half):
         if k == 2:
@@ -155,8 +151,8 @@
             z_copy(f, 0, j).start()
     norm_units(0, t + 1, 3, 4)
     norm_units(0, 6 - 2 * core, 2)
-    n_copy(0).start()
-    n_copy(1).start()
+    for j in range(3):
+        n_copy(0, j).start()
     for copy in own_copies:
         copy.wait()
     for k in range(2):
@@ -206,11 +202,15 @@
         y_copy(0, s, j).start()
         a_copy(0, s, j).start()
 
-    def pull_near(i):
-        n_copy(i).wait_recv()
-        m_copy(i).start()
-
-    crossed = ((1, 0), (2, 0), (0, 0), (0, 1))
+    def pull_near(s, j):
+        n_copy(s, j).wait_recv()
+        if s == 0:
+            n_copy(1, j).start()
+        if j == 0:
+            y_copy(3, s, 0).start()
+        a_copy(3, s, j).start()
+
+    crossed = ((1, 0), (2, 0), (3, 0), (0, 0), (0, 1))
 
     def pass_on(s):
         for f, j in crossed:
@@ -219,11 +219,8 @@
 
     def take_direct(s):
         for j in range(3):
-            for f in (1, 2):
+            for f in (1, 2, 3):
                 a_copy(f, s, j, sib).wait_recv()
-        for i in (2 * s, 2 * s + 1):
-            m_copy(i, 1 - core).wait_recv()
-        project_slots(s, 0, 1, 2)
         project_slots(s, 1, 1, 2)
         project_slots(s, 1, 3, 5)
 
@@ -232,7 +229,7 @@
             a_copy(0, s, j, sib).wait_recv()
         for f, j in crossed:
             b_copy(f, s, j, corner).wait_recv()
-        project_slots(s, 0, 2, 5)
+        project_slots(s, 0, 1, 5)
         project_slots(s, 1, 2, 3)
 
     scale = math.log2(math.e) / math.sqrt(128)
@@ -290,29 +287,27 @@
 
     for j in range(3):
         pull(0, j)
+        pull_near(0, j)
         if j == 1:
             lax.fori_loop(0, 4, project_own, 0)
     pull_diagonal(0, 0)
     pull_diagonal(0, 1)
-    n_copy(2).start()
-    pull_near(0)
-    pull_near(1)
     take_direct(0)
     pass_on(0)
     pull(1, 0)
-    n_copy(3).start()
+    pull_near(1, 0)
     take_rest(0)
     attend_away(0, 0, 1)
     pull(1, 1)
+    pull_near(1, 1)
     attend_away(0, 1, 2)
     pull_diagonal(1, 0)
     attend_away(0, 2, 3)
     pull(1, 2)
+    pull_near(1, 2)
     pull_diagonal(1, 1)
     wy_copy(2).start()
     spread((0, 1))
-    pull_near(2)
-    pull_near(3)
     attend_here(0)
     take_direct(1)
     pass_on(1)
@@ -372,6 +367,8 @@
         for j in range(3):
             for f in (1, 2):
                 z_copy(f, s, j).wait_send()
+            n_copy(s, j).wait_send()
+            for f in (1, 2, 3):
                 a_copy(f, s, j).wait_send()
         for j in range(2):
             x_copy(s, j).wait_send()
@@ -379,9 +376,6 @@
         for f, j in crossed:
             y_copy(f, s, j).wait_send()
             b_copy(f, s, j).wait_send()
-    for i in range(4):
-        n_copy(i).wait_send()
-        m_copy(i).wait_send()
     for k in range(3):
         for copy in (wy_copy, wa_copy, w0_copy) + ((wx_copy, w1_copy) if k < 2 else ()):
             copy(k).wait_send()
@@ -404,7 +398,7 @@
     vmem = pl.BlockSpec(memory_space=pltpu.VMEM)
     anywhere = pl.BlockSpec(memory_space=pl.ANY)
     pairs = [dma((2,)), dma((4,))]
-    for shape in [(2, 6), (3, 4), (3, 6), (3, 4)] + [(4,)] * 3 + [(3,)] * 5 + [(6,), (3, 2)]:
+    for shape in [(2, 6), (4, 4), (4, 6), (4, 4), (4,), (6,)] + [(3,)] * 5 + [(6,), (3, 2)]:
         pairs += [dma(shape), dma(shape)]
     return pl.pallas_call(
         layer_kernel,

time: 74.6 us -> 77.4 us (1.038)
  Pallas kernels: 72.5 us -> 75.3 us
    pallas_call x1, Pallas kernels: 72.5 us -> 75.3 us  [local(): pl.pallas_call(layer_kernel, out_shape=jax.ShapeDtypeStruct((samples, row...]
where the time goes in v6:
time: 77.4 us; the launch traced here: 77.2 us
  Pallas kernels  75.3 us (97%)
  local copies, waits for them, and re-layouts  1.87 us (2%)
    pallas_call x1, Pallas kernels, local(): pl.pallas_call(layer_kernel, out_shape=jax.ShapeDtypeStruct((samples, row...  75.3 us
    unnamed x1, local copies, waits for them, and re-layouts  1.87 us

profile of v6, /device:TPU:1, one launch (start us, length us, event | category | flops | bytes accessed | tf_op | source)
XLA Modules:
  0.0 77.2 jit_solution(13561259170849361633)
XLA Ops:
  0.0 75.3 %shard_map.91 = bf16[2,1024,128]{2,1,0:T(8,128)(2,1)} custom-call(s32[8,8]{1,0:T(8,128)} %neigh.1, s32[8]{0:T(128)} %live.1, f32[2,2,512]{2,1,0:T(2,128)} %gain.1, f32[2,2,512]{2,1,0:T(2,128)} %shift.1, bf16[16,128,512]{2,1,0:T(8,128)(2,1)} %bitcast.2, bf16[3,512,128]{2,1,0:T(8,128)(2,1)} %bitcast.3, bf16[128,512]{1,0:T(8,128)(2,1)} %wout_in.1, ...), custom_call_target="tpu_custom_call" | custom-call | tf_op jit(solution)/shard_map/pallas_call | solution.py:403
  75.3 1.9 %copy.11 = bf16[2,1024,128]{2,1,0:T(8,128)(2,1)} copy(bf16[2,1024,128]{2,1,0:T(8,128)(2,1)} %shard_map.91) | data formatting | bytes 1048576

commit v7 on v5

--- a/solution.py
+++ b/solution.py
@@ -76,39 +76,39 @@
 
         lax.fori_loop(0, count, norm_one, 0)
 
-    def unit(rank, j):
-        side = lax.div(rank, 2)
-        shared = 4 + 2 * lax.rem(rank, 2)
-        return (rank, shared + side, shared + 1 - side)[j]
+    def chunk(slot, s, owner, j):
+        u = slot * 16 + 8 * s
+        if j == 0:
+            return nrm.at[pl.ds(u + 2 * owner, 2)]
+        return nrm.at[pl.ds(u + 2 * lax.rem(owner + 2, 4) + 1, 1)]
+
+    def y_chunk(f, s, owner):
+        u = (2 + f) * 16 + 8 * s + 2 * owner
+        return nrm.at[pl.ds(u, 2 if f == 0 else 1)]
 
     def z_copy(f, s, j):
-        u = 8 * s + unit(t, j)
         return remote(
-            nrm.at[u], nrm.at[(2 + f) * 16 + u], z_s.at[f - 1, 3 * s + j],
-            z_r.at[f - 1, 3 * s + j], (minus, plus)[f - 1], t,
-        )
-
-    def x_copy(s, j):
-        u = 8 * s + unit(t, j)
+            chunk(0, s, t, j), chunk(2 + f, s, t, j), z_s.at[f - 1, 2 * s + j],
+            z_r.at[f - 1, 2 * s + j], (minus, plus)[f - 1], t,
+        )
+
+    def x_copy(s):
+        return remote(
+            chunk(3 + odd, s, t, 0), chunk(2, s, t, 0), x_s.at[s], x_r.at[s], near, t
+        )
+
+    def y_copy(f, s, owner=t):
+        ref = y_chunk(f, s, owner)
+        return remote(ref, ref, y_s.at[f, s], y_r.at[f, s], d, across)
+
+    def a_copy(f, s, j, owner=t):
+        ref = chunk(2 + f, s, owner, j)
         k = 2 * s + j
-        return remote(
-            nrm.at[(3 + odd) * 16 + u], nrm.at[2 * 16 + u], x_s.at[k], x_r.at[k], near, t
-        )
-
-    def y_copy(f, s, j, owner=t):
-        u = (2 + f) * 16 + 8 * s + unit(owner, j)
-        k = 2 * s + j
-        return remote(nrm.at[u], nrm.at[u], y_s.at[f, k], y_r.at[f, k], d, across)
-
-    def a_copy(f, s, j, owner=t):
-        u = (2 + f) * 16 + 8 * s + unit(owner, j)
-        k = 3 * s + j
-        return remote(nrm.at[u], nrm.at[u], a_s.at[f, k], a_r.at[f, k], d, sib)
-
-    def b_copy(f, s, j, owner=across):
-        u = (2 + f) * 16 + 8 * s + unit(owner, j)
-        k = 2 * s + j
-        return remote(nrm.at[u], nrm.at[u], b_s.at[f, k], b_r.at[f, k], d, sib)
+        return remote(ref, ref, a_s.at[f, k], a_r.at[f, k], d, sib)
+
+    def b_copy(f, s, owner=across):
+        ref = y_chunk(f, s, owner)
+        return remote(ref, ref, b_s.at[f, s], b_r.at[f, s], d, sib)
 
     def n_copy(i):
         u = 8 * (i // 2) + 4 * core + 2 * (i % 2)
@@ -147,14 +147,13 @@
         return remote(ref, ref, w1_s.at[k], w1_r.at[k], d, sib)
 
     state_copy(0).wait()
-    norm_units(0, t, 1)
-    norm_units(0, 4 + 2 * core, 2)
+    norm_units(0, 2 * t, 2)
     pl.semaphore_wait(barrier, 6)
-    for j in range(3):
-        for f in (1, 2):
-            z_copy(f, 0, j).start()
-    norm_units(0, t + 1, 3, 4)
-    norm_units(0, 6 - 2 * core, 2)
+    for f in (1, 2):
+        z_copy(f, 0, 0).start()
+    norm_units(0, 2 * t + 2, 6)
+    for f in (1, 2):
+        z_copy(f, 0, 1).start()
     n_copy(0).start()
     n_copy(1).start()
     for copy in own_copies:
@@ -194,46 +193,45 @@
             z_copy(f, s, j).wait_recv()
             if s == 0:
                 z_copy(f, 1, j).start()
-        if j < 2:
-            x_copy(s, j).start()
+        if j == 0:
+            x_copy(s).start()
         for f in (1, 2):
             if j == 0:
-                y_copy(f, s, 0).start()
+                y_copy(f, s).start()
             a_copy(f, s, j).start()
 
-    def pull_diagonal(s, j):
-        x_copy(s, j).wait_recv()
-        y_copy(0, s, j).start()
-        a_copy(0, s, j).start()
+    def pull_diagonal(s):
+        x_copy(s).wait_recv()
+        y_copy(0, s).start()
+        a_copy(0, s, 0).start()
 
     def pull_near(i):
         n_copy(i).wait_recv()
         m_copy(i).start()
 
-    crossed = ((1, 0), (2, 0), (0, 0), (0, 1))
+    side = lax.div(t, 2)
 
     def pass_on(s):
-        for f, j in crossed:
-            y_copy(f, s, j, across).wait_recv()
-            b_copy(f, s, j).start()
+        for f in (1, 2, 0):
+            y_copy(f, s, across).wait_recv()
+            b_copy(f, s).start()
 
     def take_direct(s):
-        for j in range(3):
+        for j in range(2):
             for f in (1, 2):
                 a_copy(f, s, j, sib).wait_recv()
         for i in (2 * s, 2 * s + 1):
             m_copy(i, 1 - core).wait_recv()
         project_slots(s, 0, 1, 2)
         project_slots(s, 1, 1, 2)
-        project_slots(s, 1, 3, 5)
+        project_slots(s, side, 3, 5)
 
     def take_rest(s):
-        for j in range(2):
-            a_copy(0, s, j, sib).wait_recv()
-        for f, j in crossed:
-            b_copy(f, s, j, corner).wait_recv()
-        project_slots(s, 0, 2, 5)
-        project_slots(s, 1, 2, 3)
+        a_copy(0, s, 0, sib).wait_recv()
+        project(2, s, side)
+        for f in (1, 2, 0):
+            b_copy(f, s, corner).wait_recv()
+        project_slots(s, 1 - side, 2, 5)
 
     scale = math.log2(math.e) / math.sqrt(128)
     lane_entry = lax.broadcasted_iota(jnp.int32, (1, KMAX * NODE_BLK), 1) // NODE_BLK
@@ -288,29 +286,25 @@
             wx_copy(w).start()
             w0_copy(w).start()
 
-    for j in range(3):
-        pull(0, j)
-        if j == 1:
-            lax.fori_loop(0, 4, project_own, 0)
-    pull_diagonal(0, 0)
-    pull_diagonal(0, 1)
+    pull(0, 0)
     n_copy(2).start()
+    lax.fori_loop(0, 4, project_own, 0)
+    pull(0, 1)
+    n_copy(3).start()
+    pull_diagonal(0)
     pull_near(0)
     pull_near(1)
     take_direct(0)
     pass_on(0)
-    pull(1, 0)
-    n_copy(3).start()
     take_rest(0)
     attend_away(0, 0, 1)
+    pull(1, 0)
+    attend_away(0, 1, 2)
     pull(1, 1)
-    attend_away(0, 1, 2)
-    pull_diagonal(1, 0)
-    attend_away(0, 2, 3)
-    pull(1, 2)
-    pull_diagonal(1, 1)
+    pull_diagonal(1)
     wy_copy(2).start()
     spread((0, 1))
+    attend_away(0, 2, 3)
     pull_near(2)
     pull_near(3)
     attend_here(0)
@@ -369,16 +363,15 @@
         finish(s)
 
     for s in range(2):
-        for j in range(3):
+        for j in range(2):
             for f in (1, 2):
                 z_copy(f, s, j).wait_send()
                 a_copy(f, s, j).wait_send()
-        for j in range(2):
-            x_copy(s, j).wait_send()
-            a_copy(0, s, j).wait_send()
-        for f, j in crossed:
-            y_copy(f, s, j).wait_send()
-            b_copy(f, s, j).wait_send()
+        x_copy(s).wait_send()
+        a_copy(0, s, 0).wait_send()
+        for f in range(3):
+            y_copy(f, s).wait_send()
+            b_copy(f, s).wait_send()
     for i in range(4):
         n_copy(i).wait_send()
         m_copy(i).wait_send()
@@ -404,7 +397,7 @@
     vmem = pl.BlockSpec(memory_space=pltpu.VMEM)
     anywhere = pl.BlockSpec(memory_space=pl.ANY)
     pairs = [dma((2,)), dma((4,))]
-    for shape in [(2, 6), (3, 4), (3, 6), (3, 4)] + [(4,)] * 3 + [(3,)] * 5 + [(6,), (3, 2)]:
+    for shape in [(2, 4), (3, 2), (3, 4), (3, 2), (2,), (4,), (4,)] + [(3,)] * 5 + [(6,), (3, 2)]:
         pairs += [dma(shape), dma(shape)]
     return pl.pallas_call(
         layer_kernel,

time: 74.6 us -> 79.9 us (1.071)
  Pallas kernels: 72.5 us -> 77.8 us
    pallas_call x1, Pallas kernels: 72.5 us -> 77.8 us  [local(): pl.pallas_call(layer_kernel, out_shape=jax.ShapeDtypeStruct((samples, row...]
where the time goes in v7:
time: 79.9 us; the launch traced here: 79.7 us
  Pallas kernels  77.8 us (97%)
  local copies, waits for them, and re-layouts  1.87 us (2%)
    pallas_call x1, Pallas kernels, local(): pl.pallas_call(layer_kernel, out_shape=jax.ShapeDtypeStruct((samples, row...  77.8 us
    unnamed x1, local copies, waits for them, and re-layouts  1.87 us

profile of v7, /device:TPU:1, one launch (start us, length us, event | category | flops | bytes accessed | tf_op | source)
XLA Modules:
  0.0 79.7 jit_solution(3720191938326804165)
XLA Ops:
  0.0 77.8 %shard_map.91 = bf16[2,1024,128]{2,1,0:T(8,128)(2,1)} custom-call(s32[8,8]{1,0:T(8,128)} %neigh.1, s32[8]{0:T(128)} %live.1, f32[2,2,512]{2,1,0:T(2,128)} %gain.1, f32[2,2,512]{2,1,0:T(2,128)} %shift.1, bf16[16,128,512]{2,1,0:T(8,128)(2,1)} %bitcast.2, bf16[3,512,128]{2,1,0:T(8,128)(2,1)} %bitcast.3, bf16[128,512]{1,0:T(8,128)(2,1)} %wout_in.1, ...), custom_call_target="tpu_custom_call" | custom-call | tf_op jit(solution)/shard_map/pallas_call | solution.py:402
  77.8 1.9 %copy.11 = bf16[2,1024,128]{2,1,0:T(8,128)(2,1)} copy(bf16[2,1024,128]{2,1,0:T(8,128)(2,1)} %shard_map.91) | data formatting | bytes 1048576

commit v8 on v5

--- a/solution.py
+++ b/solution.py
@@ -156,7 +156,6 @@
     norm_units(0, t + 1, 3, 4)
     norm_units(0, 6 - 2 * core, 2)
     n_copy(0).start()
-    n_copy(1).start()
     for copy in own_copies:
         copy.wait()
     for k in range(2):
@@ -291,19 +290,20 @@
     for j in range(3):
         pull(0, j)
         if j == 1:
+            n_copy(1).start()
             lax.fori_loop(0, 4, project_own, 0)
     pull_diagonal(0, 0)
     pull_diagonal(0, 1)
-    n_copy(2).start()
     pull_near(0)
     pull_near(1)
     take_direct(0)
     pass_on(0)
     pull(1, 0)
-    n_copy(3).start()
+    n_copy(2).start()
     take_rest(0)
     attend_away(0, 0, 1)
     pull(1, 1)
+    n_copy(3).start()
     attend_away(0, 1, 2)
     pull_diagonal(1, 0)
     attend_away(0, 2, 3)

time: 74.6 us -> 76.3 us (1.023)
  Pallas kernels: 72.5 us -> 74 us
    pallas_call x1, Pallas kernels: 72.5 us -> 74 us  [local(): pl.pallas_call(layer_kernel, out_shape=jax.ShapeDtypeStruct((samples, row...]
where the time goes in v8:
time: 76.3 us; the launch traced here: 75.9 us
  Pallas kernels  74 us (97%)
  local copies, waits for them, and re-layouts  1.87 us (2%)
    pallas_call x1, Pallas kernels, local(): pl.pallas_call(layer_kernel, out_shape=jax.ShapeDtypeStruct((samples, row...  74 us
    unnamed x1, local copies, waits for them, and re-layouts  1.87 us

profile of v8, /device:TPU:1, one launch (start us, length us, event | category | flops | bytes accessed | tf_op | source)
XLA Modules:
  0.0 75.9 jit_solution(2531033063167597106)
XLA Ops:
  0.0 74.0 %shard_map.91 = bf16[2,1024,128]{2,1,0:T(8,128)(2,1)} custom-call(s32[8,8]{1,0:T(8,128)} %neigh.1, s32[8]{0:T(128)} %live.1, f32[2,2,512]{2,1,0:T(2,128)} %gain.1, f32[2,2,512]{2,1,0:T(2,128)} %shift.1, bf16[16,128,512]{2,1,0:T(8,128)(2,1)} %bitcast.2, bf16[3,512,128]{2,1,0:T(8,128)(2,1)} %bitcast.3, bf16[128,512]{1,0:T(8,128)(2,1)} %wout_in.1, ...), custom_call_target="tpu_custom_call" | custom-call | tf_op jit(solution)/shard_map/pallas_call | solution.py:409
  74.0 1.9 %copy.11 = bf16[2,1024,128]{2,1,0:T(8,128)(2,1)} copy(bf16[2,1024,128]{2,1,0:T(8,128)(2,1)} %shard_map.91) | data formatting | bytes 1048576
